TPU v7x, 512 devices: a whole 4x8x8 slice. The times are simulated.
512 devices in a mesh: leaf: 128 (over y, z, core), sub: 4 (over x).
Axes of the slice: x: 4, y: 8, z: 8, core: 2. Of those that a mesh axis runs over, the one named last changes fastest.
Arguments:
- points: bfloat16 [16, 1048576], P(None, ('leaf', 'sub')), may hold values from -6 to 6
- basis: bfloat16 [32, 1048576], P(None, ('leaf', 'sub')), may hold values from -0.75 to 0.75
- transfer: bfloat16 [31744, 1024], P(('leaf', 'sub')), may hold values from -0.75 to 0.75
- top_transfer: bfloat16 [1024, 1024], replicated, may hold values from -0.75 to 0.75
- coupling: bfloat16 [32256, 4, 1024], P(('leaf', 'sub'))
- far_index: int32 [32256, 4], P(('leaf', 'sub')), may hold values from 0 to 16383, as said below
- far_count: int32 [32256], P(('leaf', 'sub')), may hold values from 1 to 4, as said below
- top_coupling: bfloat16 [512, 4, 1024], P(('leaf', 'sub'))
- top_index: int32 [512, 4], P(('leaf', 'sub')), may hold values from 0 to 511, as said below
- top_count: int32 [512], P(('leaf', 'sub')), may hold values from 1 to 4
- near_block: bfloat16 [16384, 4, 4096], P(('leaf', 'sub')), may hold values from -0.375 to 0.375
- near_index: int32 [16384, 4], P(('leaf', 'sub')), may hold values from 0 to 16383, as said below
- near_count: int32 [16384], P(('leaf', 'sub')), may hold values from 1 to 4, as said below
Outputs:
- hessian_product: bfloat16 [16, 1048576], P(None, ('leaf', 'sub'))
Inputs may be any that keep to these rules, and one draw needn't show every extreme that they name: `far_index`: for a cluster of a level with n = 32 >> l clusters a device, every partner lies within n of its own number. `far_count`: the first cluster of each level of each device subtree uses all slots. `top_index`: partners are nodes of the same depth within 3 positions of the node; row 0 is not read. `near_index`: slot 0 is the leaf itself; every partner lies within 32 leaves of it. `near_count`: the first leaf of each device uses all slots.
All inputs are finite; a program needn't handle non-finite values.
Results may differ from a plain program's by a relative error of at most 0.035.
Values may be sent and summed in bfloat16 or wider, within the bound.
No kernel may reach another device: no remote copies, remote signals or barrier semaphores. Data moves between devices by JAX's collectives and lax.ppermute only.
A program may use at most 64 MiB of HBM per device.

v0:
```python
import jax
import jax.numpy as jnp
from jax import lax
from jax.sharding import PartitionSpec as P

BASIS_RANK = 32
LEAF = 64
VECTOR_COUNT = 16
FAR = 4
NEAR = 4


def shifted(block, axis, distance):
    devices = range(lax.axis_size(axis))
    route = [(i - distance, i) for i in devices if i - distance in devices]
    return lax.ppermute(block, axis, route)


def climb_up(children, matrix_stack):
    halves = children.shape[0] // 2
    paired = children.reshape(halves, 2, BASIS_RANK, VECTOR_COUNT)
    joined = matrix_stack.reshape(halves, 2, BASIS_RANK, BASIS_RANK)
    parent = jnp.einsum("jckq,jckv->jqv", joined, paired, preferred_element_type=jnp.float32)
    return parent.astype(jnp.bfloat16).reshape(halves, BASIS_RANK * VECTOR_COUNT)


def descend(parent_nodes, matrix_stack, added):
    reshaped_input = matrix_stack.reshape(-1, BASIS_RANK, BASIS_RANK)
    product_output = jnp.einsum(
        "aux,axr->aur",
        reshaped_input,
        parent_nodes.reshape(-1, BASIS_RANK, VECTOR_COUNT),
        preferred_element_type=jnp.float32,
    )
    product_output = product_output + added.reshape(-1, BASIS_RANK, VECTOR_COUNT).astype(
        jnp.float32
    )
    return product_output.astype(jnp.bfloat16).reshape(-1, BASIS_RANK * VECTOR_COUNT)


def couple(blocks, partners, counts):
    slot_ids = jnp.arange(FAR, dtype=jnp.int32)
    in_use = (slot_ids[None, :] < counts[:, None]).astype(jnp.bfloat16)
    masked = partners.reshape(-1, FAR, BASIS_RANK, VECTOR_COUNT) * in_use[:, :, None, None]
    summed = jnp.einsum(
        "gfkq,gfqv->gkv",
        blocks.reshape(-1, FAR, BASIS_RANK, BASIS_RANK),
        masked,
        preferred_element_type=jnp.float32,
    )
    return summed.astype(jnp.bfloat16).reshape(-1, BASIS_RANK * VECTOR_COUNT)


def upward_top(highest, top_transfer, depth_from):
    tier_map = {depth_from: highest}
    for depth_now in range(depth_from - 1, -1, -1):
        lower_start = 1 << depth_now + 1
        tier_map[depth_now] = climb_up(
            tier_map[depth_now + 1], top_transfer[lower_start : 2 * lower_start]
        )
    return tier_map


def build_upward(shaped_basis, shaped_points, transfer, leaf_count, local_depth):
    leaf_coeff = jnp.einsum(
        "kjp,vjp->jkv", shaped_basis, shaped_points, preferred_element_type=jnp.float32
    )
    upward = [leaf_coeff.astype(jnp.bfloat16).reshape(leaf_count, BASIS_RANK * VECTOR_COUNT)]
    for height in range(local_depth):
        width_now = leaf_count >> height
        offset = 2 * leaf_count - 2 * width_now
        upward.append(climb_up(upward[height], transfer[offset : offset + width_now]))
    return upward


def local(
    points,
    basis,
    transfer,
    top_transfer,
    coupling,
    far_index,
    far_count,
    top_coupling,
    top_index,
    top_count,
    near_block,
    near_index,
    near_count,
):
    leaf_count = basis.shape[1] // LEAF
    local_depth = leaf_count.bit_length() - 1
    branch = lax.axis_size("sub")
    leaf_groups = lax.axis_size("leaf")
    subtrees = leaf_groups * branch
    depth_top = subtrees.bit_length() - 1
    device = lax.axis_index("leaf") * branch + lax.axis_index("sub")
    shaped_points = points.reshape(VECTOR_COUNT, leaf_count, LEAF)
    shaped_basis = basis.reshape(BASIS_RANK, leaf_count, LEAF)
    upward = build_upward(shaped_basis, shaped_points, transfer, leaf_count, local_depth)
    stacked = jnp.concatenate(upward, axis=0)
    lower_stack, lower_points = shifted((stacked, points), ("leaf", "sub"), 1)
    upper_stack, upper_points = shifted((stacked, points), ("leaf", "sub"), -1)
    lower_levels = []
    upper_levels = []
    for height in range(local_depth + 1):
        width_now = leaf_count >> height
        offset = 2 * leaf_count - 2 * width_now
        lower_levels.append(lower_stack[offset : offset + width_now])
        upper_levels.append(upper_stack[offset : offset + width_now])
    coupled = []
    for height in range(local_depth + 1):
        width_now = leaf_count >> height
        offset = 2 * leaf_count - 2 * width_now
        window = jnp.concatenate(
            [lower_levels[height], upward[height], upper_levels[height]], axis=0
        )
        local_ids = far_index[offset : offset + width_now] - (device - 1) * width_now
        partners = window[local_ids]
        coupled.append(
            couple(
                coupling[offset : offset + width_now],
                partners,
                far_count[offset : offset + width_now],
            )
        )
    root_row = upward[local_depth]
    all_roots = lax.all_gather(root_row, ("leaf", "sub"), axis=0, tiled=True)
    tier_map = upward_top(all_roots, top_transfer, depth_top)
    heap_rows = jnp.concatenate(
        [jnp.zeros((1, BASIS_RANK * VECTOR_COUNT), jnp.bfloat16)]
        + [tier_map[depth_now] for depth_now in range(depth_top)],
        axis=0,
    )
    own_coupled = couple(top_coupling, heap_rows[top_index], top_count)
    all_coupled = lax.all_gather(own_coupled, ("leaf", "sub"), axis=0, tiled=True)
    carried = all_coupled[1:2]
    own_node = subtrees + device
    for depth_now in range(1, depth_top):
        ancestor = jnp.right_shift(own_node, depth_top - depth_now)
        carried = descend(
            carried,
            lax.dynamic_slice_in_dim(top_transfer, ancestor, 1, 0),
            lax.dynamic_slice_in_dim(all_coupled, ancestor, 1, 0),
        )
    carried = descend(
        carried, lax.dynamic_slice_in_dim(top_transfer, own_node, 1, 0), coupled[local_depth]
    )
    for height in range(local_depth - 1, -1, -1):
        width_now = leaf_count >> height
        offset = 2 * leaf_count - 2 * width_now
        carried = descend(
            jnp.repeat(carried, 2, axis=0), transfer[offset : offset + width_now], coupled[height]
        )
    far_part = jnp.einsum(
        "kjp,jkv->vjp",
        shaped_basis,
        carried.reshape(leaf_count, BASIS_RANK, VECTOR_COUNT),
        preferred_element_type=jnp.float32,
    )
    window_points = jnp.concatenate([lower_points, points, upper_points], axis=1).reshape(
        VECTOR_COUNT, 3 * leaf_count, LEAF
    )
    local_leaves = near_index - (device - 1) * leaf_count
    in_use = (jnp.arange(NEAR, dtype=jnp.int32)[None, :] < near_count[:, None]).astype(jnp.bfloat16)
    gathered = window_points[:, local_leaves] * in_use[None, :, :, None]
    near_part = jnp.einsum(
        "tfpq,vtfq->vtp",
        near_block.reshape(leaf_count, NEAR, LEAF, LEAF),
        gathered,
        preferred_element_type=jnp.float32,
    )
    return (far_part + near_part).astype(jnp.bfloat16).reshape(VECTOR_COUNT, leaf_count * LEAF)


def solution(mesh):
    placed = (
        P(None, ("leaf", "sub")),
        P(None, ("leaf", "sub")),
        P(("leaf", "sub"), None),
        P(),
        P(("leaf", "sub"), None, None),
        P(("leaf", "sub"), None),
        P(("leaf", "sub")),
        P(("leaf", "sub"), None, None),
        P(("leaf", "sub"), None),
        P(("leaf", "sub")),
        P(("leaf", "sub"), None, None),
        P(("leaf", "sub"), None),
        P(("leaf", "sub")),
    )
    return jax.shard_map(
        local, mesh=mesh, in_specs=placed, out_specs=P(None, ("leaf", "sub")), check_vma=False
    )
```

profile of v0, /device:TPU:1, one launch (start us, length us, event | category | flops | bytes accessed | tf_op | source)
XLA Modules:
  0.0 405.6 jit_solution(4090443520517764755)
XLA Ops:
  3.8 1.2 reshape.579
  9.5 2.4 concatenate.28
  11.9 3.9 collective-permute-start
  15.9 3.7 collective-permute-start.1
  19.6 1.9 collective-permute-start.2
  21.6 4.9 %collective-permute-start.3 = (bf16[16,2048]{1,0:T(8,128)(2,1)}, bf16[16,2048]{1,0:T(8,128)(2,1)}, u32[]{:S(2)}, u32[]{:S(2)}) collective-permute-start(bf16[16,2048]{1,0:T(8,128)(2,1)} %param.13), channel_id=1, source_target_pairs={{1,0},{2,1},{3,2},{4,3},{5,4},{6,5},{7,6},{8,7},{9,8},{10,9},{11,1... | collective-permute-start | bytes 196616 | tf_op jit(solution)/shard_map/ppermute | solution.py:16
  34.9 135.7 %all-gather = bf16[512,1,512]{2,1,0:T(2,128)(2,1)S(1)} all-gather(bf16[1,1,512]{2,1,0:T(2,128)(2,1)S(1)} %reshape.727), channel_id=1, replica_groups=mesh['leaf'=128,'sub'=4] {'leaf','sub'}, dimensions={0}, use_global_device_ids=true | all-gather | bytes 525312 | tf_op jit(solution)/shard_map/all_gather | solution.py:128
  170.6 3.2 reduce.9
  173.8 4.7 %reshape.587 = bf16[256,2,32,16]{3,2,1,0:T(8,128)(2,1)} reshape(bf16[512,512]{1,0:T(8,128)(2,1)S(1)} %reduce.9) | data formatting | bytes 1048576 | tf_op jit(solution)/shard_map/reshape | solution.py:21
  178.4 4.4 %reshape.588 = bf16[256,2,32,32]{3,2,1,0:T(8,128)(2,1)} reshape(bf16[512,1024]{1,0:T(8,128)(2,1)S(1)} %slice-done) | data formatting | bytes 2097152 | tf_op jit(solution)/shard_map/reshape | solution.py:22
  182.8 2.9 reshape.589
  185.8 1.8 reshape.590
  187.6 1.2 reshape.591
  190.7 4.7 %bitcast_convert_fusion = bf16[256,16,32]{2,1,0:T(8,128)(2,1)S(1)} fusion(bf16[256,2,32,16]{3,2,1,0:T(8,128)(2,1)} %reshape.587, bf16[256,2,32,32]{3,2,1,0:T(8,128)(2,1)} %reshape.588), kind=kOutput, calls=%fused_computation.8 | convolution fusion | flops 16908288 | bytes 1835008 | tf_op jit(solution)/shard_map/jckq,jckv->jqv/dot_general | solution.py:23
  202.0 1.8 copy.90
  203.8 1.1 copy.94
  207.9 124.2 %all-gather.1 = bf16[512,1,512]{2,1,0:T(2,128)(2,1)S(1)} all-gather(bf16[1,1,512]{2,1,0:T(2,128)(2,1)S(1)} %reshape.729), channel_id=1, replica_groups=mesh['leaf'=128,'sub'=4] {'leaf','sub'}, dimensions={0}, use_global_device_ids=true | all-gather | bytes 525312 | tf_op jit(solution)/shard_map/all_gather | solution.py:136
  348.1 1.2 compare_convert_fusion
  351.0 1.3 fusion.100
  355.0 1.1 reshape.628
  356.1 1.3 fusion.72
  357.6 1.6 reshape.632
  360.1 1.6 reshape.634
  361.7 1.4 fusion.71
  374.5 1.1 fusion.32
  379.4 1.2 fusion.26
  388.4 1.1 fusion.14
  389.5 1.2 fusion.15
  393.5 1.5 gather_fusion.6
  395.0 2.7 reshape.631
  397.7 2.5 fusion.6
  400.3 1.5 fusion.9
  (318 shorter events, 77.8 us)
Async XLA Ops:
  6.7 19.8 %copy-start.17 = (bf16[2,32,32]{2,1,0:T(8,128)(2,1)}, bf16[2,32,32]{2,1,0:T(8,128)(2,1)S(1)}, u32[]{:S(2)}) copy-start(bf16[2,32,32]{2,1,0:T(8,128)(2,1)S(1)} %reshape.585) | copy-start | bytes 12292
  6.9 19.6 %copy-start.2 = (bf16[1024,1024]{1,0:T(8,128)(2,1)S(1)}, bf16[1024,1024]{1,0:T(8,128)(2,1)}, u32[]{:S(2)}) copy-start(bf16[1024,1024]{1,0:T(8,128)(2,1)} %param.16) | copy-start | bytes 6291460
  8.5 18.9 %copy-start.32 = (bf16[1,512]{1,0:T(2,128)(2,1)}, bf16[1,512]{1,0:T(2,128)(2,1)S(1)}, u32[]{:S(2)}) copy-start(bf16[1,512]{1,0:T(2,128)(2,1)S(1)} %reshape.586) | copy-start | bytes 3076
  8.6 18.8 %copy-start.31 = (bf16[2,512]{1,0:T(2,128)(2,1)}, bf16[2,512]{1,0:T(2,128)(2,1)S(1)}, u32[]{:S(2)}) copy-start(bf16[2,512]{1,0:T(2,128)(2,1)S(1)} %reshape.613) | copy-start | bytes 6148
  8.8 18.6 %copy-start.26 = (bf16[4,512]{1,0:T(4,128)(2,1)}, bf16[4,512]{1,0:T(4,128)(2,1)S(1)}, u32[]{:S(2)}) copy-start(bf16[4,512]{1,0:T(4,128)(2,1)S(1)} %reshape.612) | copy-start | bytes 12292
  9.1 18.4 %copy-start.23 = (bf16[8,512]{1,0:T(8,128)(2,1)}, bf16[8,512]{1,0:T(8,128)(2,1)S(1)}, u32[]{:S(2)}) copy-start(bf16[8,512]{1,0:T(8,128)(2,1)S(1)} %reshape.611) | copy-start | bytes 24580
  9.4 18.0 %copy-start.19 = (bf16[16,512]{1,0:T(8,128)(2,1)}, bf16[16,512]{1,0:T(8,128)(2,1)S(1)}, u32[]{:S(2)}) copy-start(bf16[16,512]{1,0:T(8,128)(2,1)S(1)} %reshape.610) | copy-start | bytes 49156
  9.5 18.0 %copy-start.12 = (bf16[32,512]{1,0:T(8,128)(2,1)}, bf16[32,512]{1,0:T(8,128)(2,1)S(1)}, u32[]{:S(2)}) copy-start(bf16[32,512]{1,0:T(8,128)(2,1)S(1)} %copy.111) | copy-start | bytes 98308
  11.9 355.7 %collective-permute-start = (bf16[63,512]{1,0:T(8,128)(2,1)}, bf16[63,512]{1,0:T(8,128)(2,1)}, u32[]{:S(2)}, u32[]{:S(2)}) collective-permute-start(bf16[63,512]{1,0:T(8,128)(2,1)} %concatenate.28), channel_id=1, source_target_pairs={{0,1},{1,2},{2,3},{3,4},{4,5},{5,6},{6,7},{7,8},{8,9},{9,10},{10,1... | collective-permute-start | bytes 193544 | tf_op jit(solution)/shard_map/ppermute | solution.py:16
  15.9 352.5 %collective-permute-start.1 = (bf16[63,512]{1,0:T(8,128)(2,1)}, bf16[63,512]{1,0:T(8,128)(2,1)}, u32[]{:S(2)}, u32[]{:S(2)}) collective-permute-start(bf16[63,512]{1,0:T(8,128)(2,1)} %concatenate.28), channel_id=1, source_target_pairs={{1,0},{2,1},{3,2},{4,3},{5,4},{6,5},{7,6},{8,7},{9,8},{10,9},{11,1... | collective-permute-start | bytes 193544 | tf_op jit(solution)/shard_map/ppermute | solution.py:16
  19.6 382.2 %collective-permute-start.2 = (bf16[16,2048]{1,0:T(8,128)(2,1)}, bf16[16,2048]{1,0:T(8,128)(2,1)}, u32[]{:S(2)}, u32[]{:S(2)}) collective-permute-start(bf16[16,2048]{1,0:T(8,128)(2,1)} %param.13), channel_id=1, source_target_pairs={{0,1},{1,2},{2,3},{3,4},{4,5},{5,6},{6,7},{7,8},{8,9},{9,10},{10,1... | collective-permute-start | bytes 196616 | tf_op jit(solution)/shard_map/ppermute | solution.py:16
  21.6 380.3 %collective-permute-start.3 = (bf16[16,2048]{1,0:T(8,128)(2,1)}, bf16[16,2048]{1,0:T(8,128)(2,1)}, u32[]{:S(2)}, u32[]{:S(2)}) collective-permute-start(bf16[16,2048]{1,0:T(8,128)(2,1)} %param.13), channel_id=1, source_target_pairs={{1,0},{2,1},{3,2},{4,3},{5,4},{6,5},{7,6},{8,7},{9,8},{10,9},{11,1... | collective-permute-start | bytes 196616 | tf_op jit(solution)/shard_map/ppermute | solution.py:16
  202.0 131.0 %copy-start.3 = (bf16[1024,1024]{1,0:T(8,128)(2,1)S(1)}, bf16[1024,1024]{1,0:T(8,128)(2,1)}, u32[]{:S(2)}) copy-start(bf16[1024,1024]{1,0:T(8,128)(2,1)} %param.16) | copy-start | bytes 6291460
  202.0 143.1 %copy-start.25 = (s32[63,4]{0,1:T(4,128)S(1)}, s32[63,4]{0,1:T(4,128)}, u32[]{:S(2)}) copy-start(s32[63,4]{0,1:T(4,128)} %param.18) | copy-start | bytes 3028
  202.0 143.8 %slice-start.6 = ((bf16[63,4,1024]{2,1,0:T(4,128)(2,1)}), bf16[1,4,1024]{2,1,0:T(4,128)(2,1)S(1)}, s32[]{:S(2)}) async-start(bf16[63,4,1024]{2,1,0:T(4,128)(2,1)} %param.17), calls=%async_computation.6 | async-start | bytes 16384 | tf_op jit(solution)/shard_map/slice | solution.py:122
  203.8 143.6 %slice-start.7 = ((bf16[63,4,1024]{2,1,0:T(4,128)(2,1)}), bf16[2,4,1024]{2,1,0:T(4,128)(2,1)S(1)}, s32[]{:S(2)}) async-start(bf16[63,4,1024]{2,1,0:T(4,128)(2,1)} %param.17), calls=%async_computation.7 | async-start | bytes 32768 | tf_op jit(solution)/shard_map/slice | solution.py:122
  203.8 146.4 %slice-start.8 = ((bf16[63,4,1024]{2,1,0:T(4,128)(2,1)}), bf16[4,4,1024]{2,1,0:T(4,128)(2,1)S(1)}, s32[]{:S(2)}) async-start(bf16[63,4,1024]{2,1,0:T(4,128)(2,1)} %param.17), calls=%async_computation.8 | async-start | bytes 65536 | tf_op jit(solution)/shard_map/slice | solution.py:122
  203.8 149.4 %slice-start.9 = ((bf16[63,4,1024]{2,1,0:T(4,128)(2,1)}), bf16[8,4,1024]{2,1,0:T(4,128)(2,1)S(1)}, s32[]{:S(2)}) async-start(bf16[63,4,1024]{2,1,0:T(4,128)(2,1)} %param.17), calls=%async_computation.9 | async-start | bytes 131072 | tf_op jit(solution)/shard_map/slice | solution.py:122
  203.8 150.3 %copy-start.39 = (s32[8]{0:T(128)S(1)}, s32[8]{0:T(128)}, u32[]{:S(2)}) copy-start(s32[8]{0:T(128)} %slice.173) | copy-start | bytes 100
  203.8 151.2 %slice-start.10 = ((bf16[63,4,1024]{2,1,0:T(4,128)(2,1)}), bf16[16,4,1024]{2,1,0:T(4,128)(2,1)S(1)}, s32[]{:S(2)}) async-start(bf16[63,4,1024]{2,1,0:T(4,128)(2,1)} %param.17), calls=%async_computation.10 | async-start | bytes 262144 | tf_op jit(solution)/shard_map/slice | solution.py:122
  205.6 151.7 %copy-start.36 = (s32[32,4]{0,1:T(4,128)S(1)}, s32[32,4]{0,1:T(4,128)}, u32[]{:S(2)}) copy-start(s32[32,4]{0,1:T(4,128)} %param.24) | copy-start | bytes 1540
  207.9 151.3 %copy-start.38 = (s32[63]{0:T(128)S(1)}, s32[63]{0:T(128)}, u32[]{:S(2)}) copy-start(s32[63]{0:T(128)} %param.19) | copy-start | bytes 760
  332.2 25.4 %slice-start.11 = ((bf16[63,4,1024]{2,1,0:T(4,128)(2,1)}), bf16[32,4,1024]{2,1,0:T(4,128)(2,1)S(1)}, s32[]{:S(2)}) async-start(bf16[63,4,1024]{2,1,0:T(4,128)(2,1)} %param.17), calls=%async_computation.11 | async-start | bytes 524288 | tf_op jit(solution)/shard_map/slice | solution.py:122
  333.1 27.0 %copy-start.6 = (bf16[32,4,4096]{2,1,0:T(4,128)(2,1)S(1)}, bf16[32,4,4096]{2,1,0:T(4,128)(2,1)}, u32[]{:S(2)}) copy-start(bf16[32,4,4096]{2,1,0:T(4,128)(2,1)} %param.23) | copy-start | bytes 3145732
  359.1 17.5 %copy-start.18 = (bf16[2,32,32]{2,1,0:T(8,128)(2,1)S(1)}, bf16[2,32,32]{2,1,0:T(8,128)(2,1)}, u32[]{:S(2)}) copy-start(bf16[2,32,32]{2,1,0:T(8,128)(2,1)} %copy-done.17) | copy-start | bytes 12292
  359.1 19.4 %copy-start.27 = (bf16[4,512]{1,0:T(4,128)(2,1)S(1)}, bf16[4,512]{1,0:T(4,128)(2,1)}, u32[]{:S(2)}) copy-start(bf16[4,512]{1,0:T(4,128)(2,1)} %copy-done.26) | copy-start | bytes 12292
  360.0 20.6 %copy-start.21 = (bf16[4,32,32]{2,1,0:T(8,128)(2,1)S(1)}, bf16[4,32,32]{2,1,0:T(8,128)(2,1)}, u32[]{:S(2)}) copy-start(bf16[4,32,32]{2,1,0:T(8,128)(2,1)} %reshape.618) | copy-start | bytes 24580
  360.0 22.5 %copy-start.24 = (bf16[8,512]{1,0:T(8,128)(2,1)S(1)}, bf16[8,512]{1,0:T(8,128)(2,1)}, u32[]{:S(2)}) copy-start(bf16[8,512]{1,0:T(8,128)(2,1)} %copy-done.23) | copy-start | bytes 24580
  360.0 23.5 %copy-start.15 = (bf16[8,4,32,32]{3,2,1,0:T(8,128)(2,1)S(1)}, bf16[8,4,32,32]{3,2,1,0:T(8,128)(2,1)}, u32[]{:S(2)}) copy-start(bf16[8,4,32,32]{3,2,1,0:T(8,128)(2,1)} %reshape.624) | copy-start | bytes 196612
  361.7 22.8 %copy-start.14 = (bf16[8,32,32]{2,1,0:T(8,128)(2,1)S(1)}, bf16[8,32,32]{2,1,0:T(8,128)(2,1)}, u32[]{:S(2)}) copy-start(bf16[8,32,32]{2,1,0:T(8,128)(2,1)} %reshape.622) | copy-start | bytes 49156
  361.7 25.5 %copy-start.20 = (bf16[16,512]{1,0:T(8,128)(2,1)S(1)}, bf16[16,512]{1,0:T(8,128)(2,1)}, u32[]{:S(2)}) copy-start(bf16[16,512]{1,0:T(8,128)(2,1)} %copy-done.19) | copy-start | bytes 49156
  377.7 10.6 %copy-start.11 = (bf16[16,4,32,32]{3,2,1,0:T(8,128)(2,1)S(1)}, bf16[16,4,32,32]{3,2,1,0:T(8,128)(2,1)}, u32[]{:S(2)}) copy-start(bf16[16,4,32,32]{3,2,1,0:T(8,128)(2,1)} %reshape.628) | copy-start | bytes 393220
  (25 other events, 118.1 us)
where the time goes:
time: 408 us; the launch traced here: 406 us
  blocking collectives  260 us (64%)
  local copies, waits for them, and re-layouts  88.5 us (22%)
  matrix products  25.4 us (6%)
  other arithmetic  15.6 us (4%)
  starting transfers between devices  14.5 us (4%)
    all_gather x1, blocking collectives, local(): all_roots = lax.all_gather(root_row, ('leaf', 'sub'), axis=0, tiled=True)  136 us
    all_gather x1, blocking collectives, local(): lax.all_gather(own_coupled, ('leaf', 'sub'), axis=0, tiled=True)  124 us
    ppermute x4, starting transfers between devices, shifted(): return lax.ppermute(block, axis, route)  14.5 us
    reshape x12, local copies, waits for them, and re-layouts, climb_up(): joined = matrix_stack.reshape(halves, 2, BASIS_RANK, BASIS_RANK)  12.5 us
    dot_general x14, matrix products, climb_up(): jnp.einsum('jckq,jckv->jqv', joined, paired, preferred_element_type=jnp.f...  8.27 us
  transfers between devices with their start and end apart: 4, of which 0 were waited for; matrix products, arithmetic and copies ran while one was open for 28% of the time, Pallas kernels for 0%

commit v1 on v0

v1 whole, which is shorter than its diff:
```python
import jax
import jax.numpy as jnp
import numpy as np
from jax import lax
from jax.experimental import pallas as pl
from jax.experimental.pallas import tpu as pltpu
from jax.sharding import Mesh
from jax.sharding import PartitionSpec as P

RANK = 32
LEAF = 64
VEC = 16
FAR = 4
NEAR = 4
LPD = 32
LEVELS = 6
OFFS = [2 * LPD - 2 * (LPD >> h) for h in range(LEVELS)]
ALL = ("y", "z", "core", "x")
PLANE = ("z", "core", "x")
REACH = 3
TAPS = 2 * REACH + 1
MSG = 160
SIZES = [(1 << d) + 2 * REACH for d in range(6)] + [8 + 6, 16 + 6, 32 + 6]
STARTS = [sum(SIZES[:d]) for d in range(9)]
NODES = sum(SIZES)
F32 = jnp.float32
BF16 = jnp.bfloat16

_l = np.arange(128)
_c = np.arange(1024)
SPREAD = (_l[:, None] == _c[None, :] // 32).astype(np.float32)
FOLD = (_l[:, None] % 32 == _l[None, :] % 32).astype(np.float32)
GATHER = (_c[:, None] // 32 == _l[None, :] % 32).astype(np.float32)
PICK = np.concatenate(
    [FOLD * (_l[:, None] // 32 == q) for q in range(4)], axis=1
)
HALF = np.concatenate(
    [
        ((_l[:, None] // 64 == h) & (_l[:, None] % 64 == _l[None, :] % 64)).astype(np.float32)
        for h in range(2)
    ],
    axis=1,
)
_p = np.arange(4096)
NEARSUM = (_p[:, None] // 64 == np.arange(256)[None, :] % 64).astype(np.float32)


def const(a):
    return jnp.asarray(a, BF16)


def dot(a, b):
    return jnp.dot(a, b, preferred_element_type=F32)


def lanes(shape, width):
    return lax.broadcasted_iota(jnp.int32, shape, len(shape) - 1) // width


def up_level(c, e, spread, fold, n):
    x = dot(c, spread)
    out = []
    for p in range(n // 2):
        t = x[32 * p : 32 * p + 16] * e[2 * p : 2 * p + 1]
        t = t + x[32 * p + 16 : 32 * p + 32] * e[2 * p + 1 : 2 * p + 2]
        q = t[:, 0:128]
        for m in range(1, 8):
            q = q + t[:, 128 * m : 128 * m + 128]
        out.append(q)
    q = jnp.concatenate(out, 0) if len(out) > 1 else out[0]
    return dot(q.astype(BF16), fold).astype(BF16)


def pack(c):
    m = c.shape[0] // 32
    c = c.reshape(m, 4, 8, 128)
    g = lanes((m, 8, 128), 32)
    r = jnp.where(
        g == 0, c[:, 0], jnp.where(g == 1, c[:, 1], jnp.where(g == 2, c[:, 2], c[:, 3]))
    )
    return r.reshape(m * 8, 128)


def unpack(r, pick):
    m = r.shape[0] // 8
    w = dot(r, pick)
    parts = [w[:, 128 * q : 128 * q + 128].reshape(m, 1, 8, 128) for q in range(4)]
    return jnp.concatenate(parts, 1).reshape(m * 32, 128)


def block_basis(basis, i):
    b = basis[:, 256 * i : 256 * i + 256]
    b = jnp.concatenate([b] * 4, 0)
    rows = lax.broadcasted_iota(jnp.int32, (128, 256), 0) // 32
    return jnp.where(rows == lanes((128, 256), 64), b, jnp.zeros_like(b))


def up_kernel(points, basis, transfer, spread, fold, root_out, stack_out, ex_out):
    pts = points[...]
    bas = basis[...].astype(F32)
    e = transfer[...].astype(F32)
    rows = []
    g = lanes((16, 128), 32)
    for i in range(8):
        bd = block_basis(bas, i).astype(BF16)
        c = lax.dot_general(
            pts[:, 256 * i : 256 * i + 256],
            bd,
            (((1,), (1,)), ((), ())),
            preferred_element_type=F32,
        )
        for k in range(4):
            rows.append(jnp.where(g == k, c, 0.0))
    c = dot(jnp.concatenate(rows, 0).astype(BF16), fold[...]).astype(BF16)
    levels = [c]
    for h in range(LEVELS - 1):
        n = LPD >> h
        c = up_level(c, e[OFFS[h] : OFFS[h] + n], spread[...], fold[...], n)
        levels.append(c)
    root = c.astype(F32)
    g8 = lanes((8, 128), 32)
    msg = jnp.where(g8 == 0, root[0:8], jnp.where(g8 == 1, root[8:16], 0.0))
    msg = jnp.concatenate([msg, msg], 0).astype(BF16)
    for i in range(32):
        root_out[16 * i : 16 * i + 16] = msg
    stack = jnp.concatenate(levels + [jnp.zeros((16, 128), BF16)], 0)
    stack_out[...] = stack
    ex_out[0:256] = pack(stack.astype(F32)).astype(BF16)
    for i in range(16):
        ex_out[256 + 16 * i : 272 + 16 * i] = pts[:, 128 * i : 128 * i + 128]


def plane_kernel(slots, arrived, rows, tops, spread, fold, pick, msg_out, own_out):
    w = dot(arrived[...], pick[:, 0:256])
    c = jnp.concatenate(
        [w[:, 0:128].reshape(64, 1, 8, 128), w[:, 128:256].reshape(64, 1, 8, 128)], 1
    )
    c = c.reshape(1024, 128).astype(BF16)
    e = rows[...].astype(F32)
    levels = []
    at = 0
    n = 64
    while n > 1:
        c = up_level(c, e[at : at + n], spread[...], fold[...], n)
        levels.append(c)
        at += n
        n //= 2
    d8, d7, d6, d5, d4, d3 = levels
    own_out[0:128] = d6
    own_out[128:384] = d7
    own_out[384:896] = d8
    last = [d6[80:128], d7[208:256], d8[464:512]]
    nodes = [d3, d4, d5, d6[0:48], d7[0:48], d8[0:48]] + last + [jnp.zeros((16, 128), BF16)]
    packed = pack(jnp.concatenate(nodes, 0).astype(F32))
    b = tops[...].astype(F32)
    taps = []
    for o in range(TAPS):
        t = jnp.zeros((8, 128), F32)
        for f in range(FAR):
            t = t + jnp.where(slots[f] == o, b[8 * f : 8 * f + 8], 0.0)
        taps.append(t)
    msg = jnp.concatenate(taps + [packed], 0).astype(BF16)
    for p in range(8):
        msg_out[MSG * p : MSG * p + MSG] = msg


def top_kernel(at, arrived, own, rows, spread, fold, pick, gather, out, table):
    table[...] = jnp.zeros((NODES * 16, 128), F32)

    def put(depth, place, value):
        s = (STARTS[depth] + place) * 16
        table[s : s + value.shape[0]] = value

    d3 = []
    for p in range(8):
        c = unpack(arrived[MSG * p + 48 : MSG * p + 96][8:40], pick[...])
        d3.append(c[0:16])
        put(4, REACH + 2 * p, c[16:48])
        put(5, REACH + 4 * p, c[48:112])
    c = jnp.concatenate(d3, 0)
    put(3, REACH, c)
    c = c.astype(BF16)
    e = rows[...].astype(F32)
    c = up_level(c, e[0:8], spread[...], fold[...], 8)
    put(2, REACH, c.astype(F32))
    c = up_level(c, e[8:12], spread[...], fold[...], 4)
    put(1, REACH, c.astype(F32))
    c = up_level(c, e[12:14], spread[...], fold[...], 2)
    put(0, REACH, c.astype(F32))
    prior = unpack(arrived[pl.ds(pl.multiple_of(at[0] * MSG, 16), MSG)][80:160], pick[...])
    later = unpack(arrived[pl.ds(pl.multiple_of(at[1] * MSG, 16), MSG)][80:160], pick[...])
    mine = own[...].astype(F32)
    for i, n in enumerate((8, 16, 32)):
        put(6 + i, REACH + n, later[16 * (1 + 3 * i) : 16 * (4 + 3 * i)])
        put(6 + i, 0, prior[16 * (10 + 3 * i) : 16 * (13 + 3 * i)])
        begin = 16 * (n - 8)
        put(6 + i, REACH, mine[begin : begin + 16 * n])
    sums = []
    for s in range(4):
        taps = arrived[pl.ds(pl.multiple_of(at[2 + s] * MSG, 16), MSG)][0:64].astype(F32)
        acc = [None] * 8
        for o in range(TAPS):
            c = table[pl.ds(pl.multiple_of((at[6 + s] + o) * 16, 16), 16)]
            for m in range(8):
                t = taps[8 * o + m : 8 * o + m + 1] * c
                acc[m] = t if o == 0 else acc[m] + t
        sums.append(jnp.concatenate(acc, 1))
    z = dot(jnp.concatenate(sums, 0).astype(BF16), gather[...])
    z = pack(z).astype(BF16)
    for i in range(64):
        out[16 * i : 16 * i + 16] = z


def couple_kernel(idx, before, stack, after, coupling, pick, gather, out, table, prod):
    table[0:1024] = unpack(before[0:256], pick[...])
    table[1024:2048] = stack[...].astype(F32)
    table[2048:3072] = unpack(after[0:256], pick[...])
    prod[1008:1024] = jnp.zeros((16, 1024), BF16)

    @pl.loop(0, 63, unroll=3)
    def _(t):
        b = coupling[t].astype(F32)
        acc = [None] * 8
        for f in range(FAR):
            c = table[pl.ds(pl.multiple_of(idx[t, f], 16), 16)]
            for m in range(8):
                r = b[f : f + 1, 128 * m : 128 * m + 128] * c
                acc[m] = r if f == 0 else acc[m] + r
        prod[pl.ds(pl.multiple_of(t * 16, 16), 16)] = jnp.concatenate(acc, 1).astype(BF16)

    out[...] = dot(prod[...], gather[...]).astype(BF16)


def near_kernel(idx, before, points, after, block, half, nearsum, out, table, prod):
    window = [before[256:512]]
    window += [points[:, 128 * i : 128 * i + 128] for i in range(16)]
    window += [after[256:512]]
    w = dot(jnp.concatenate(window, 0), half[...])
    w = jnp.concatenate(
        [w[:, 0:128].reshape(48, 1, 16, 128), w[:, 128:256].reshape(48, 1, 16, 128)], 1
    )
    table[0:1536] = w.reshape(1536, 128)
    table[1536:1552] = jnp.zeros((16, 128), F32)

    @pl.loop(0, LPD)
    def _(t):
        b = block[t].astype(F32)
        c = [table[pl.ds(pl.multiple_of(idx[t, f], 16), 16)] for f in range(NEAR)]
        acc = []
        for m in range(32):
            s = slice(128 * m, 128 * m + 128)
            r = b[0:1, s] * c[0]
            for f in range(1, NEAR):
                r = r + b[f : f + 1, s] * c[f]
            acc.append(r.astype(BF16))
        prod[pl.ds(pl.multiple_of(t * 16, 16), 16)] = jnp.concatenate(acc, 1)

    r = dot(prod[...], nearsum[...])
    g = lanes((16, 256), 64)
    for i in range(8):
        t = r[64 * i : 64 * i + 16]
        for k in range(1, 4):
            t = jnp.where(g == k, r[64 * i + 16 * k : 64 * i + 16 * k + 16], t)
        out[:, 256 * i : 256 * i + 256] = t


def down_kernel(at, arrived, rows, zl, transfer, basis, near, pick, gather, out):
    got = [arrived[pl.ds(pl.multiple_of(at[d] * 16, 16), 16)] for d in range(9)]
    first = [unpack(got[d][0:8], pick[...]) for d in range(7)]
    second = [unpack(got[d][8:16], pick[...]) for d in (7, 8)]
    z = [first[d][0:16] for d in range(6)]
    z += [first[6][16:32], second[0][0:16], second[1][16:32]]
    zloc = zl[...].astype(F32)
    z.append(zloc[992:1008])
    e = rows[...].astype(F32)

    def spread_down(y, row):
        return jnp.concatenate([y * row[:, 128 * m : 128 * m + 128] for m in range(8)], 1)

    y = z[0]
    for d in range(1, 10):
        t = spread_down(y, e[d - 1 : d]).astype(BF16)
        y = (dot(t, gather[...]) + z[d]).astype(BF16).astype(F32)
    e = transfer[...].astype(F32)
    for h in range(LEVELS - 2, -1, -1):
        n = LPD >> h
        t = [
            spread_down(y[16 * (j // 2) : 16 * (j // 2) + 16], e[OFFS[h] + j : OFFS[h] + j + 1])
            for j in range(n)
        ]
        t = jnp.concatenate(t, 0).astype(BF16)
        zs = zloc[16 * OFFS[h] : 16 * (OFFS[h] + n)]
        y = (dot(t, gather[...]) + zs).astype(BF16).astype(F32)
    bas = basis[...].astype(F32)
    g = lanes((16, 128), 32)
    for i in range(8):
        t = y[64 * i : 64 * i + 16]
        for k in range(1, 4):
            t = jnp.where(g == k, y[64 * i + 16 * k : 64 * i + 16 * k + 16], t)
        s = slice(256 * i, 256 * i + 256)
        far = dot(t.astype(BF16), block_basis(bas, i).astype(BF16))
        out[:, s] = (far + near[:, s]).astype(BF16)


def call(kernel, out, scratch, n_smem, args, flops, moved):
    specs = [pl.BlockSpec(memory_space=pltpu.SMEM)] * n_smem
    specs += [pl.BlockSpec(memory_space=pltpu.VMEM)] * (len(args) - n_smem)
    outs = jax.tree.map(lambda s: pl.BlockSpec(memory_space=pltpu.VMEM), out)
    return pl.pallas_call(
        kernel,
        out_shape=out,
        in_specs=specs,
        out_specs=outs,
        scratch_shapes=scratch,
        compiler_params=pltpu.CompilerParams(vmem_limit_bytes=48 << 20),
        cost_estimate=pl.CostEstimate(flops=flops, bytes_accessed=moved, transcendentals=0),
    )(*args)


def shape(rows, cols, dtype=BF16):
    return jax.ShapeDtypeStruct((rows, cols), dtype)


def local(
    points,
    basis,
    transfer,
    top_transfer,
    coupling,
    far_index,
    far_count,
    top_coupling,
    top_index,
    top_count,
    near_block,
    near_index,
    near_count,
):
    y = lax.axis_index("y")
    device = lax.axis_index(ALL)
    low = device % 64
    spread, fold, gather, pick = const(SPREAD), const(FOLD), const(GATHER), const(PICK)
    half, nearsum = const(HALF), const(NEARSUM)

    root_msg, stack, ex = call(
        up_kernel,
        (shape(512, 128), shape(1024, 128), shape(512, 128)),
        [],
        0,
        (points, basis, transfer, spread, fold),
        200_000_000,
        2_000_000,
    )
    plane_roots = lax.all_to_all(root_msg, PLANE, 0, 0, tiled=True)
    devices = 512
    before = lax.ppermute(ex, ALL, [(i, i + 1) for i in range(devices - 1)])
    after = lax.ppermute(ex, ALL, [(i + 1, i) for i in range(devices - 1)])

    ids = [(n << 3) + y * n + jnp.arange(n) for n in (64, 32, 16, 8, 4, 2)]
    ids += [jnp.arange(8, 16), jnp.arange(4, 8), jnp.arange(2, 4)]
    ids += [jnp.right_shift(devices + device, 9 - jnp.arange(1, 10)), jnp.zeros((3,), jnp.int32)]
    top_rows = top_transfer[jnp.concatenate([i.astype(jnp.int32) for i in ids])]

    tap = top_index[0] - device + REACH
    live = (jnp.arange(FAR, dtype=jnp.int32) < top_count[0]) & (device > 0)
    tap = jnp.where(live, tap, -1)
    msg, own = call(
        plane_kernel,
        (shape(8 * MSG, 128), shape(896, 128)),
        [],
        1,
        (
            tap,
            plane_roots,
            top_rows[0:126],
            top_coupling.reshape(32, 128),
            spread,
            fold,
            pick,
        ),
        300_000_000,
        2_000_000,
    )
    planes = lax.all_to_all(msg, "y", 0, 0, tiled=True)

    slot_plane = jnp.stack([0 * y, 0 * y + 1, 2 + y // 4, 4 + y // 2])
    depth = sum((low >= (1 << d)).astype(jnp.int32) for d in range(1, 6))
    starts = jnp.asarray(np.array(STARTS[:6], np.int32))
    place = jnp.stack(
        [
            starts[depth] + jnp.where(low > 0, low - jnp.left_shift(1, depth), 0),
            STARTS[6] + low % 8,
            STARTS[7] + low % 16,
            STARTS[8] + low % 32,
        ]
    )
    at = jnp.concatenate(
        [jnp.stack([jnp.maximum(y - 1, 0), jnp.minimum(y + 1, 7)]), slot_plane, place]
    ).astype(jnp.int32)
    z_msg = call(
        top_kernel,
        shape(1024, 128),
        [pltpu.VMEM((NODES * 16, 128), F32)],
        1,
        (at, planes, own, top_rows[126:140], spread, fold, pick, gather),
        200_000_000,
        2_000_000,
    )
    z_all = lax.all_to_all(z_msg, PLANE, 0, 0, tiled=True)

    where_near = near_index - (device - 1) * LPD
    used = jnp.arange(NEAR, dtype=jnp.int32)[None, :] < near_count[:, None]
    near_at = jnp.where(used, where_near, 3 * LPD) * 16
    near = call(
        near_kernel,
        shape(VEC, LPD * LEAF, F32),
        [pltpu.VMEM((1552, 128), F32), pltpu.VMEM((512, 4096), BF16)],
        1,
        (near_at, before, points, after, near_block, half, nearsum),
        2_000_000_000,
        8_000_000,
    )

    width = np.concatenate([np.full(LPD >> h, LPD >> h) for h in range(LEVELS)])
    offset = np.concatenate([np.full(LPD >> h, OFFS[h]) for h in range(LEVELS)])
    width = jnp.asarray(width[:, None].astype(np.int32))
    offset = jnp.asarray(offset[:, None].astype(np.int32))
    inside = far_index - (device - 1) * width
    used = jnp.arange(FAR, dtype=jnp.int32)[None, :] < far_count[:, None]
    which = (inside >= width).astype(jnp.int32) + (inside >= 2 * width).astype(jnp.int32)
    far_at = jnp.where(used, which * 64 + offset + inside - which * width, 63 + 64) * 16
    zl = call(
        couple_kernel,
        shape(1024, 128),
        [pltpu.VMEM((3072, 128), F32), pltpu.VMEM((1024, 1024), BF16)],
        1,
        (far_at, before, stack, after, coupling, pick, gather),
        1_000_000_000,
        6_000_000,
    )

    source = jnp.right_shift(devices + device, 9 - jnp.arange(9)).astype(jnp.int32) % 64
    return call(
        down_kernel,
        shape(VEC, LPD * LEAF),
        [],
        1,
        (source, z_all, top_rows[140:149], zl, transfer, basis, near, pick, gather),
        300_000_000,
        2_000_000,
    )


def solution(mesh):
    grid = Mesh(mesh.devices.reshape(8, 8, 2, 4), ALL)
    one, two, three = P(ALL), P(ALL, None), P(ALL, None, None)
    wide = P(None, ALL)
    placed = (wide, wide, two, P(), three, two, one, three, two, one, three, two, one)
    return jax.shard_map(local, mesh=grid, in_specs=placed, out_specs=wide, check_vma=False)
```

time: 408 us -> 92.6 us (0.23)
  blocking collectives: 260 us -> 0 us
  local copies, waits for them, and re-layouts: 88.5 us -> 13.5 us
  matrix products: 25.4 us -> 0 us
  starting transfers between devices: 14.5 us -> 39.3 us
  Pallas kernels: 0 us -> 22.9 us
  other arithmetic: 15.6 us -> 0.26 us
  waiting for transfers between devices: 0.01 us -> 14.1 us
    all_gather x2 -> x0, blocking collectives: 260 us -> none  [the longest x1 136 us: local(): all_roots = lax.all_gather(root_row, ('leaf', 'sub'), axis=0, tiled=True)]
    reshape x53 -> x1, local copies, waits for them, and re-layouts: 38.3 us -> 0.01 us  [local(): top_coupling.reshape(32, 128)]
    all_to_all x0 -> x3, starting transfers between devices: none -> 31.4 us  [the longest x1 16.1 us: local(): plane_roots = lax.all_to_all(root_msg, PLANE, 0, 0, tiled=True)]
    dot_general x33 -> x0, matrix products: 25.4 us -> none  [the longest x14 8.27 us: climb_up(): jnp.einsum('jckq,jckv->jqv', joined, paired, preferred_element_type=jnp.f...]
    pallas_call x0 -> x6, Pallas kernels: none -> 22.9 us  [call(): pl.pallas_call(kernel, out_shape=out, in_specs=specs, out_specs=outs, scr...]
    slice x51 -> x3, local copies, waits for them, and re-layouts: 17.7 us -> 2.62 us  [the longest x1 0.97 us: local(): top_rows[0:126]]
    all_to_all x0 -> x3, waiting for transfers between devices: none -> 14.1 us  [the longest x1 8.77 us: local(): planes = lax.all_to_all(msg, 'y', 0, 0, tiled=True)]
    convert_element_type x37 -> x0, local copies, waits for them, and re-layouts: 10.6 us -> none  [the longest x16 5.97 us: descend(): added.reshape(-1, BASIS_RANK, VECTOR_COUNT).astype(jnp.float32)]
  transfers between devices with their start and end apart: 4 -> 5, of which waited for: 0 -> 2; matrix products, arithmetic and copies ran while one was open for 28% -> 6% of each run, Pallas kernels for 0% -> 18%
where the time goes in v1:
time: 92.6 us; the launch traced here: 91.8 us
  starting transfers between devices  39.3 us (42%)
  Pallas kernels  22.9 us (25%)
  waiting for transfers between devices  14.1 us (15%)
  local copies, waits for them, and re-layouts  13.5 us (15%)
  between operations  1.85 us (2%)
    pallas_call x6, Pallas kernels, call(): pl.pallas_call(kernel, out_shape=out, in_specs=specs, out_specs=outs, scr...  22.9 us
    all_to_all x1, starting transfers between devices, local(): plane_roots = lax.all_to_all(root_msg, PLANE, 0, 0, tiled=True)  16.1 us
    all_to_all x1, waiting for transfers between devices, local(): planes = lax.all_to_all(msg, 'y', 0, 0, tiled=True)  8.77 us
    all_to_all x1, starting transfers between devices, local(): z_all = lax.all_to_all(z_msg, PLANE, 0, 0, tiled=True)  8.51 us
    unnamed x61, local copies, waits for them, and re-layouts  8.26 us
    all_to_all x1, starting transfers between devices, local(): planes = lax.all_to_all(msg, 'y', 0, 0, tiled=True)  6.83 us
    ppermute x1, starting transfers between devices, local(): after = lax.ppermute(ex, ALL, [(i + 1, i) for i in range(devices - 1)])  5.91 us
    all_to_all x1, waiting for transfers between devices, local(): plane_roots = lax.all_to_all(root_msg, PLANE, 0, 0, tiled=True)  5.3 us
  transfers between devices with their start and end apart: 5, of which 2 were waited for; matrix products, arithmetic and copies ran while one was open for 6% of the time, Pallas kernels for 18%

profile of v1, /device:TPU:1, one launch (start us, length us, event | category | flops | bytes accessed | tf_op | source)
XLA Modules:
  0.0 91.8 jit_solution(3238196643767735832)
XLA Ops:
  0.0 1.1 %copy-done.3 = bf16[128,1024]{1,0:T(8,128)(2,1)S(1)} copy-done((bf16[128,1024]{1,0:T(8,128)(2,1)S(1)}, bf16[128,1024]{1,0:T(8,128)(2,1)}, u32[]{:S(2)}) %copy-start.3) | copy-done | bytes 262168
  1.1 0.9 copy-done.5
  2.0 0.9 copy-done.7
  2.9 0.8 copy-done.9
  3.7 0.8 copy-done.13
  4.5 2.7 %shard_map.208 = (bf16[512,128]{1,0:T(8,128)(2,1)}, bf16[1024,128]{1,0:T(8,128)(2,1)S(1)}, bf16[512,128]{1,0:T(8,128)(2,1)}) custom-call(bf16[16,2048]{1,0:T(8,128)(2,1)S(1)} %copy-done.13, bf16[32,2048]{1,0:T(8,128)(2,1)S(1)} %copy-done.5, bf16[62,1024]{1,0:T(8,128)(2,1)S(1)} %copy-done.7, bf16[128,1024]{1,0:T(8,128)(2,1)S(1)} %copy-done.3, ...), custom_call_target="tpu_custom_call" | custom-call | flops 200000000 | bytes 2000000 | tf_op jit(solution)/shard_map/pallas_call | solution.py:309
  7.2 0.7 copy-done.17
  7.9 5.9 %collective-permute-start.1 = (bf16[512,128]{1,0:T(8,128)(2,1)}, bf16[512,128]{1,0:T(8,128)(2,1)}, u32[]{:S(2)}, u32[]{:S(2)}) collective-permute-start(bf16[512,128]{1,0:T(8,128)(2,1)} %get-tuple-element.13), channel_id=1, source_target_pairs={{1,0},{2,1},{3,2},{4,3},{5,4},{6,5},{7,6},{8,7},{9,8},{10,9},{11,1... | collective-permute-start | bytes 393224 | tf_op jit(solution)/shard_map/ppermute | solution.py:357
  13.8 1.9 %collective-permute-start = (bf16[512,128]{1,0:T(8,128)(2,1)}, bf16[512,128]{1,0:T(8,128)(2,1)}, u32[]{:S(2)}, u32[]{:S(2)}) collective-permute-start(bf16[512,128]{1,0:T(8,128)(2,1)} %get-tuple-element.13), channel_id=1, source_target_pairs={{0,1},{1,2},{2,3},{3,4},{4,5},{5,6},{6,7},{7,8},{8,9},{9,10},{10,1... | collective-permute-start | bytes 393224 | tf_op jit(solution)/shard_map/ppermute | solution.py:356
  15.8 16.1 %all-to-all-start = ((bf16[64,8,128]{2,1,0:T(8,128)(2,1)}), bf16[64,8,128]{2,1,0:T(8,128)(2,1)S(1)}, u32[]{:S(2)}, u32[]{:S(2)}) async-start(bf16[64,8,128]{2,1,0:T(8,128)(2,1)} %bitcast.11), calls=%async_computation | async-start | bytes 262144 | tf_op jit(solution)/shard_map/all_to_all | solution.py:354
  32.0 0.1 concatenate.59
  32.3 1.7 %gather_fusion = bf16[152,1024]{1,0:T(8,128)(2,1)} fusion(bf16[1024,1024]{1,0:T(8,128)(2,1)S(1)} %copy-done, s32[1024]{0:T(1024)S(1)} %pad_clamp_fusion), kind=kCustom, calls=%fused_computation | custom fusion | bytes 623200 | tf_op jit(solution)/shard_map/gather | solution.py:362
  34.0 0.8 slice.15.rows
  34.8 1.0 %slice.14.rows = bf16[126,1024]{1,0:T(8,128)(2,1)S(1)} slice(bf16[152,1024]{1,0:T(8,128)(2,1)} %gather_fusion), slice={[0:126], [0:1024]} | slice | bytes 516096 | tf_op jit(solution)/shard_map/slice | solution.py:375
  36.5 5.3 %all-to-all-done = bf16[64,8,128]{2,1,0:T(8,128)(2,1)S(1)} async-done(((bf16[64,8,128]{2,1,0:T(8,128)(2,1)}), bf16[64,8,128]{2,1,0:T(8,128)(2,1)S(1)}, u32[]{:S(2)}, u32[]{:S(2)}) %all-to-all-start) | async-done | bytes 131104 | tf_op jit(solution)/shard_map/all_to_all | solution.py:354
  41.8 3.8 %shard_map.209 = (bf16[1280,128]{1,0:T(8,128)(2,1)}, bf16[896,128]{1,0:T(8,128)(2,1)S(1)}) custom-call(s32[4]{0:T(128)S(1)} %and_select_fusion.slots, bf16[512,128]{1,0:T(8,128)(2,1)S(1)} %bitcast.44, bf16[126,1024]{1,0:T(8,128)(2,1)S(1)} %slice.14.rows, bf16[32,128]{1,0:T(8,128)(2,1)S(1)} %reshape.263.tops, bf16[128,1024]{1,0:T(8,128)(2,1)S(1)} %copy-done.4, ...), custom_call_target="tpu_custom_call" | custom-call | flops 300000000 | bytes 2000000 | tf_op jit(solution)/shard_map/pallas_call | solution.py:309
  45.6 6.8 %all-to-all-start.1 = ((bf16[8,160,128]{2,1,0:T(8,128)(2,1)}), bf16[8,160,128]{2,1,0:T(8,128)(2,1)S(1)}, u32[]{:S(2)}, u32[]{:S(2)}) async-start(bf16[8,160,128]{2,1,0:T(8,128)(2,1)} %bitcast.24), calls=%async_computation.1 | async-start | bytes 655360 | tf_op jit(solution)/shard_map/all_to_all | solution.py:384
  52.5 0.1 copy.28
  52.5 0.1 copy.26
  52.7 0.6 dynamic_slice.3
  53.9 0.1 concatenate.47.at
  54.1 0.1 select_multiply_fusion.idx
  54.2 8.8 %all-to-all-done.1 = bf16[8,160,128]{2,1,0:T(8,128)(2,1)S(1)} async-done(((bf16[8,160,128]{2,1,0:T(8,128)(2,1)}), bf16[8,160,128]{2,1,0:T(8,128)(2,1)S(1)}, u32[]{:S(2)}, u32[]{:S(2)}) %all-to-all-start.1) | async-done | bytes 327712 | tf_op jit(solution)/shard_map/all_to_all | solution.py:384
  63.0 2.7 %shard_map.210 = bf16[1024,128]{1,0:T(8,128)(2,1)} custom-call(s32[10]{0:T(128)S(1)} %concatenate.47.at, bf16[1280,128]{1,0:T(8,128)(2,1)S(1)} %bitcast.42, bf16[896,128]{1,0:T(8,128)(2,1)S(1)} %get-tuple-element.12.own, bf16[14,1024]{1,0:T(8,128)(2,1)S(1)} %slice.15.rows, bf16[128,1024]{1,0:T(8,128)(2,1)S(1)} %copy-done.4, bf16[128,128]{1,0:T(8,128)(2,1)S(1)} %copy-done.10, ...), custom_call_target="tpu_custom_call" | custom-call | flops 200000000 | bytes 2000000 | tf_op jit(solution)/shard_map/pallas_call | solution.py:309
  65.6 8.5 %all-to-all-start.2 = ((bf16[64,16,128]{2,1,0:T(8,128)(2,1)}), bf16[64,16,128]{2,1,0:T(8,128)(2,1)S(1)}, u32[]{:S(2)}, u32[]{:S(2)}) async-start(bf16[64,16,128]{2,1,0:T(8,128)(2,1)} %bitcast.26), calls=%async_computation.2 | async-start | bytes 524288 | tf_op jit(solution)/shard_map/all_to_all | solution.py:409
  74.3 0.8 slice.16.rows
  75.2 1.0 %copy-done.12 = bf16[63,4,1024]{2,1,0:T(4,128)(2,1)S(1)} copy-done((bf16[63,4,1024]{2,1,0:T(4,128)(2,1)S(1)}, bf16[63,4,1024]{2,1,0:T(4,128)(2,1)}, u32[]{:S(2)}) %copy-start.12) | copy-done | bytes 516120
  76.2 0.9 %copy-done.18 = bf16[1024,128]{1,0:T(8,128)(2,1)S(1)} copy-done((bf16[1024,128]{1,0:T(8,128)(2,1)S(1)}, bf16[1024,128]{1,0:T(8,128)(2,1)}, u32[]{:S(2)}) %copy-start.18) | copy-done | bytes 262168
  77.1 3.7 %shard_map.211.zl = bf16[1024,128]{1,0:T(8,128)(2,1)S(1)} custom-call(s32[63,4]{1,0:T(8,128)S(1)} %select_multiply_fusion.idx, bf16[512,128]{1,0:T(8,128)(2,1)} %collective-permute-done.before, bf16[1024,128]{1,0:T(8,128)(2,1)S(1)} %copy-done.18, bf16[512,128]{1,0:T(8,128)(2,1)} %collective-permute-done.1.after, bf16[63,4,1024]{2,1,0:T(4,128)(2,1)S(1)} %copy-done.12, ...), custom_call_target="tpu_custom_call" | custom-call | flops 1000000000 | bytes 6000000 | tf_op jit(solution)/shard_map/pallas_call | solution.py:309
  80.9 0.8 copy-done.16
  81.7 6.0 %shard_map.212.near = f32[16,2048]{1,0:T(8,128)S(1)} custom-call(s32[32,4]{1,0:T(8,128)S(1)} %select_multiply_fusion.1.idx, bf16[512,128]{1,0:T(8,128)(2,1)} %collective-permute-done.before, bf16[16,2048]{1,0:T(8,128)(2,1)S(1)} %copy-done.14, bf16[512,128]{1,0:T(8,128)(2,1)} %collective-permute-done.1.after, bf16[32,4,4096]{2,1,0:T(4,128)(2,1)S(1)} %copy-done.11, ...), custom_call_target="tpu_custom_call" | custom-call | flops 2000000000 | bytes 8000000 | tf_op jit(solution)/shard_map/pallas_call | solution.py:309
  87.8 4.0 %shard_map.213 = bf16[16,2048]{1,0:T(8,128)(2,1)} custom-call(s32[9]{0:T(128)S(1)} %and_select_fusion.1.at, bf16[1024,128]{1,0:T(8,128)(2,1)S(1)} %bitcast.43, bf16[9,1024]{1,0:T(8,128)(2,1)S(1)} %slice.16.rows, bf16[1024,128]{1,0:T(8,128)(2,1)S(1)} %shard_map.211.zl, bf16[62,1024]{1,0:T(8,128)(2,1)S(1)} %copy-done.8, bf16[32,2048]{1,0:T(8,128)(2,1)S(1)} %copy-done.6, ...), custom_call_target="tpu_custom_call" | custom-call | flops 300000000 | bytes 2000000 | tf_op jit(solution)/shard_map/pallas_call | solution.py:309
  (70 shorter events, 0.3 us)
Async XLA Ops:
  0.0 32.2 %copy-start = (bf16[1024,1024]{1,0:T(8,128)(2,1)S(1)}, bf16[1024,1024]{1,0:T(8,128)(2,1)}, u32[]{:S(2)}) copy-start(bf16[1024,1024]{1,0:T(8,128)(2,1)} %param.25) | copy-start | bytes 6291460
  0.0 1.1 %copy-start.3 = (bf16[128,1024]{1,0:T(8,128)(2,1)S(1)}, bf16[128,1024]{1,0:T(8,128)(2,1)}, u32[]{:S(2)}) copy-start(bf16[128,1024]{1,0:T(8,128)(2,1)} %constant.154.clone.spread) | copy-start | bytes 786436
  1.1 0.9 copy-start.5
  2.0 0.9 copy-start.7
  7.9 28.6 %copy-start.19 = (bf16[1,4,1024]{2,1,0:T(4,128)(2,1)S(1)}, bf16[1,4,1024]{2,1,0:T(4,128)(2,1)}, u32[]{:S(2)}) copy-start(bf16[1,4,1024]{2,1,0:T(4,128)(2,1)} %param.29) | copy-start | bytes 24580
  7.9 28.6 %copy-start.27 = (s32[1,4]{1,0:T(1,128)S(1)}, s32[1,4]{1,0:T(1,128)}, u32[]{:S(2)}) copy-start(s32[1,4]{1,0:T(1,128)} %param.30) | copy-start | bytes 52
  7.9 33.9 %copy-start.2 = (bf16[128,512]{1,0:T(8,128)(2,1)S(1)}, bf16[128,512]{1,0:T(8,128)(2,1)}, u32[]{:S(2)}) copy-start(bf16[128,512]{1,0:T(8,128)(2,1)} %constant.157.clone.pick) | copy-start | bytes 393220
  7.9 33.9 %copy-start.4 = (bf16[128,1024]{1,0:T(8,128)(2,1)S(1)}, bf16[128,1024]{1,0:T(8,128)(2,1)}, u32[]{:S(2)}) copy-start(bf16[128,1024]{1,0:T(8,128)(2,1)} %constant.154.clone.spread) | copy-start | bytes 786436
  7.9 33.9 %copy-start.10 = (bf16[128,128]{1,0:T(8,128)(2,1)S(1)}, bf16[128,128]{1,0:T(8,128)(2,1)}, u32[]{:S(2)}) copy-start(bf16[128,128]{1,0:T(8,128)(2,1)} %constant.155.clone.fold) | copy-start | bytes 98308
  7.9 67.2 %collective-permute-start.1 = (bf16[512,128]{1,0:T(8,128)(2,1)}, bf16[512,128]{1,0:T(8,128)(2,1)}, u32[]{:S(2)}, u32[]{:S(2)}) collective-permute-start(bf16[512,128]{1,0:T(8,128)(2,1)} %get-tuple-element.13), channel_id=1, source_target_pairs={{1,0},{2,1},{3,2},{4,3},{5,4},{6,5},{7,6},{8,7},{9,8},{10,9},{11,1... | collective-permute-start | bytes 393224 | tf_op jit(solution)/shard_map/ppermute | solution.py:357
  13.8 61.3 %collective-permute-start = (bf16[512,128]{1,0:T(8,128)(2,1)}, bf16[512,128]{1,0:T(8,128)(2,1)}, u32[]{:S(2)}, u32[]{:S(2)}) collective-permute-start(bf16[512,128]{1,0:T(8,128)(2,1)} %get-tuple-element.13), channel_id=1, source_target_pairs={{0,1},{1,2},{2,3},{3,4},{4,5},{5,6},{6,7},{7,8},{8,9},{9,10},{10,1... | collective-permute-start | bytes 393224 | tf_op jit(solution)/shard_map/ppermute | solution.py:356
  15.8 26.0 %all-to-all-start = ((bf16[64,8,128]{2,1,0:T(8,128)(2,1)}), bf16[64,8,128]{2,1,0:T(8,128)(2,1)S(1)}, u32[]{:S(2)}, u32[]{:S(2)}) async-start(bf16[64,8,128]{2,1,0:T(8,128)(2,1)} %bitcast.11), calls=%async_computation | async-start | bytes 262144 | tf_op jit(solution)/shard_map/all_to_all | solution.py:354
  32.2 20.2 %copy-start.21 = (s32[32,4]{0,1:T(4,128)S(1)}, s32[32,4]{0,1:T(4,128)}, u32[]{:S(2)}) copy-start(s32[32,4]{0,1:T(4,128)} %param.33) | copy-start | bytes 1540
  32.2 20.3 %copy-start.20 = (s32[63,4]{0,1:T(4,128)S(1)}, s32[63,4]{0,1:T(4,128)}, u32[]{:S(2)}) copy-start(s32[63,4]{0,1:T(4,128)} %param.27) | copy-start | bytes 3028
  32.2 20.4 %copy-start.29 = (s32[6]{0:T(128)S(1)}, s32[6]{0:T(128)}, u32[]{:S(2)}) copy-start(s32[6]{0:T(128)} %constant.160.clone) | copy-start | bytes 76
  32.2 21.8 %copy-start.28 = (s32[63,1]{0,1:T(1,128)S(1)}, s32[63,1]{0,1:T(1,128)}, u32[]{:S(2)}) copy-start(s32[63,1]{0,1:T(1,128)} %constant.161.clone) | copy-start | bytes 760
  32.3 21.8 %copy-start.22 = (s32[63]{0:T(128)S(1)}, s32[63]{0:T(128)}, u32[]{:S(2)}) copy-start(s32[63]{0:T(128)} %param.28) | copy-start | bytes 760
  32.3 21.8 %copy-start.24 = (s32[63]{0:T(128)S(1)}, s32[63]{0:T(128)}, u32[]{:S(2)}) copy-start(s32[63]{0:T(128)} %constant.176) | copy-start | bytes 760
  32.3 21.8 %copy-start.25 = (s32[63]{0:T(128)S(1)}, s32[63]{0:T(128)}, u32[]{:S(2)}) copy-start(s32[63]{0:T(128)} %constant.175) | copy-start | bytes 760
  32.3 21.8 %copy-start.26 = (s32[63]{0:T(128)S(1)}, s32[63]{0:T(128)}, u32[]{:S(2)}) copy-start(s32[63]{0:T(128)} %constant.173) | copy-start | bytes 760
  32.3 30.6 %copy-start.1 = (bf16[1024,128]{1,0:T(8,128)(2,1)S(1)}, bf16[1024,128]{1,0:T(8,128)(2,1)}, u32[]{:S(2)}) copy-start(bf16[1024,128]{1,0:T(8,128)(2,1)} %constant.156.clone.gather) | copy-start | bytes 786436
  35.8 38.4 %copy-start.23 = (s32[32]{0:T(128)S(1)}, s32[32]{0:T(128)}, u32[]{:S(2)}) copy-start(s32[32]{0:T(128)} %param.34) | copy-start | bytes 388
  45.6 17.3 %all-to-all-start.1 = ((bf16[8,160,128]{2,1,0:T(8,128)(2,1)}), bf16[8,160,128]{2,1,0:T(8,128)(2,1)S(1)}, u32[]{:S(2)}, u32[]{:S(2)}) async-start(bf16[8,160,128]{2,1,0:T(8,128)(2,1)} %bitcast.24), calls=%async_computation.1 | async-start | bytes 655360 | tf_op jit(solution)/shard_map/all_to_all | solution.py:384
  65.6 15.2 %copy-start.14 = (bf16[16,2048]{1,0:T(8,128)(2,1)S(1)}, bf16[16,2048]{1,0:T(8,128)(2,1)}, u32[]{:S(2)}) copy-start(bf16[16,2048]{1,0:T(8,128)(2,1)} %points.3) | copy-start | bytes 196612
  65.6 22.1 %all-to-all-start.2 = ((bf16[64,16,128]{2,1,0:T(8,128)(2,1)}), bf16[64,16,128]{2,1,0:T(8,128)(2,1)S(1)}, u32[]{:S(2)}, u32[]{:S(2)}) async-start(bf16[64,16,128]{2,1,0:T(8,128)(2,1)} %bitcast.26), calls=%async_computation.2 | async-start | bytes 524288 | tf_op jit(solution)/shard_map/all_to_all | solution.py:409
  74.2 6.7 %copy-start.11 = (bf16[32,4,4096]{2,1,0:T(4,128)(2,1)S(1)}, bf16[32,4,4096]{2,1,0:T(4,128)(2,1)}, u32[]{:S(2)}) copy-start(bf16[32,4,4096]{2,1,0:T(4,128)(2,1)} %block.1) | copy-start | bytes 3145732
  75.1 1.0 %copy-start.12 = (bf16[63,4,1024]{2,1,0:T(4,128)(2,1)S(1)}, bf16[63,4,1024]{2,1,0:T(4,128)(2,1)}, u32[]{:S(2)}) copy-start(bf16[63,4,1024]{2,1,0:T(4,128)(2,1)} %coupling.1) | copy-start | bytes 1548292
  76.2 0.9 %copy-start.18 = (bf16[1024,128]{1,0:T(8,128)(2,1)S(1)}, bf16[1024,128]{1,0:T(8,128)(2,1)}, u32[]{:S(2)}) copy-start(bf16[1024,128]{1,0:T(8,128)(2,1)} %copy-done.17) | copy-start | bytes 786436
  77.1 3.7 %copy-start.15 = (bf16[4096,256]{1,0:T(8,128)(2,1)S(1)}, bf16[4096,256]{1,0:T(8,128)(2,1)}, u32[]{:S(2)}) copy-start(bf16[4096,256]{1,0:T(8,128)(2,1)} %constant.159.clone.nearsum) | copy-start | bytes 6291460
  80.9 0.8 copy-start.16
  81.7 6.0 %copy-start.6 = (bf16[32,2048]{1,0:T(8,128)(2,1)S(1)}, bf16[32,2048]{1,0:T(8,128)(2,1)}, u32[]{:S(2)}) copy-start(bf16[32,2048]{1,0:T(8,128)(2,1)} %basis.3) | copy-start | bytes 393220
  81.7 6.0 %copy-start.8 = (bf16[62,1024]{1,0:T(8,128)(2,1)S(1)}, bf16[62,1024]{1,0:T(8,128)(2,1)}, u32[]{:S(2)}) copy-start(bf16[62,1024]{1,0:T(8,128)(2,1)} %transfer.3) | copy-start | bytes 380932
  (3 other events, 2.3 us)

commit v2 on v1

v2 whole, which is shorter than its diff:
```python
import jax
import jax.numpy as jnp
import numpy as np
from jax import lax
from jax.experimental import pallas as pl
from jax.experimental.pallas import tpu as pltpu
from jax.sharding import Mesh
from jax.sharding import PartitionSpec as P

RANK = 32
LEAF = 64
VEC = 16
FAR = 4
NEAR = 4
LPD = 32
LEVELS = 6
OFFS = [2 * LPD - 2 * (LPD >> h) for h in range(LEVELS)]
ALL = ("y", "z", "core", "x")
PLANE = ("z", "core", "x")
REACH = 3
TAPS = 2 * REACH + 1
MSG = 176
SIZES = [(1 << d) + 2 * REACH for d in range(6)] + [8 + 6, 16 + 6, 32 + 6]
STARTS = [sum(SIZES[:d]) for d in range(9)]
NODES = sum(SIZES)
VMEM_LIMIT = 56 << 20
COST = (4, 1, 4, 3, 8, 4, 4)
F32 = jnp.float32
BF16 = jnp.bfloat16

_l = np.arange(128)
def dot(a, b):
    return jnp.dot(a, b, preferred_element_type=F32)


def lanes(shape, width):
    return lax.broadcasted_iota(jnp.int32, shape, len(shape) - 1) // width


def up_level(c, e, spread, n):
    x = dot(c, spread)
    out = []
    row = (lambda i: e[i]) if isinstance(e, list) else (lambda i: e[i : i + 1])
    for p in range(n // 2):
        t = x[32 * p : 32 * p + 16] * row(2 * p)
        t = t + x[32 * p + 16 : 32 * p + 32] * row(2 * p + 1)
        q = t[:, 0:128]
        for m in range(1, 8):
            q = q + t[:, 128 * m : 128 * m + 128]
        out.append(q)
    q = jnp.concatenate(out, 0) if len(out) > 1 else out[0]
    return q.astype(BF16)


def up_levels(c, rows):
    first, rest, fold = spread_matrix(False), spread_matrix(True), fold_matrix()
    levels = []
    n = c.shape[0] // 16
    for i, e in enumerate(rows):
        c = up_level(c, e, first if i == 0 else rest, n)
        levels.append(dot(c, fold).astype(BF16))
        n //= 2
    return levels


def pack(c):
    m = c.shape[0] // 32
    c = c.reshape(m, 4, 8, 128)
    g = lanes((m, 8, 128), 32)
    r = jnp.where(
        g == 0, c[:, 0], jnp.where(g == 1, c[:, 1], jnp.where(g == 2, c[:, 2], c[:, 3]))
    )
    return r.reshape(m * 8, 128)


def unpack(r, pick):
    m = r.shape[0] // 8
    w = dot(r, pick)
    parts = [w[:, 128 * q : 128 * q + 128].reshape(m, 1, 8, 128) for q in range(4)]
    return jnp.concatenate(parts, 1).reshape(m * 32, 128)


def block_basis(basis, i):
    b = basis[:, 256 * i : 256 * i + 256]
    b = jnp.concatenate([b] * 4, 0)
    rows = lax.broadcasted_iota(jnp.int32, (128, 256), 0) // 32
    return jnp.where(rows == lanes((128, 256), 64), b, jnp.zeros_like(b))


def iota(shape, axis, width):
    return lax.broadcasted_iota(jnp.int32, shape, axis) // width


def mask(cond):
    return jnp.where(cond, 1.0, 0.0).astype(BF16)


def spread_matrix(parts):
    r = iota((128, 1024), 0, 1)
    return mask(iota((128, 1024), 1, 32) == (r % 32 if parts else r))


def fold_matrix():
    return mask((iota((128, 128), 1, 1) - iota((128, 128), 0, 1)) % 32 == 0)


def gather_matrix():
    return mask((iota((1024, 128), 0, 32) - iota((1024, 128), 1, 1)) % 32 == 0)


def pick_matrix():
    r, c = iota((128, 512), 0, 1), iota((128, 512), 1, 1)
    return mask(((r - c) % 32 == 0) & (r // 32 == c // 128))


def pair_matrix():
    r, c = iota((256, 128), 0, 1), iota((256, 128), 1, 1)
    return mask(r % 128 // 4 * 2 + r // 128 == c % 64)


def position():
    low = (lax.axis_index("z") * 2 + lax.axis_index("core")) * 4 + lax.axis_index("x")
    return lax.axis_index("y"), low


def up_kernel(ready, points, basis, transfer, root_out, stack_out):
    fold = fold_matrix()
    ready()
    pts = points[...]
    bas = basis[...].astype(F32)
    e = transfer[...].astype(F32)
    rows = []
    g = lanes((16, 128), 32)
    for i in range(8):
        bd = block_basis(bas, i).astype(BF16)
        c = lax.dot_general(
            pts[:, 256 * i : 256 * i + 256],
            bd,
            (((1,), (1,)), ((), ())),
            preferred_element_type=F32,
        )
        for k in range(4):
            rows.append(jnp.where(g == k, c, 0.0))
    c = dot(jnp.concatenate(rows, 0).astype(BF16), fold).astype(BF16)
    below = [e[OFFS[h] : OFFS[h] + (LPD >> h)] for h in range(LEVELS - 1)]
    levels = [c] + up_levels(c, below)
    root = levels[-1].astype(F32)
    g8 = lanes((8, 128), 32)
    msg = jnp.where(g8 == 0, root[0:8], jnp.where(g8 == 1, root[8:16], 0.0))
    msg = jnp.concatenate([msg, msg], 0).astype(BF16)
    for i in range(32):
        root_out[16 * i : 16 * i + 16] = msg
    stack_out[...] = jnp.concatenate(levels + [jnp.zeros((16, 128), BF16)], 0)


def exchange_kernel(ready, stack, points, ex_out):
    ready()
    ex_out[0:256] = pack(stack[...].astype(F32)).astype(BF16)
    for i in range(16):
        ex_out[256 + 16 * i : 272 + 16 * i] = points[:, 128 * i : 128 * i + 128]


def plane_kernel(ready, index, count, arrived, rows, tops, msg_out, own_out, low_rows):
    pick = pick_matrix()
    y, low = position()
    node = y * 64 + low
    ready()
    w = dot(arrived[...], pick[:, 0:256])
    c = jnp.concatenate(
        [w[:, 0:128].reshape(64, 1, 8, 128), w[:, 128:256].reshape(64, 1, 8, 128)], 1
    )
    c = c.reshape(1024, 128).astype(BF16)
    low_rows[...] = rows[0][...].astype(F32)
    e = [rows[3][...].astype(F32), rows[2][...].astype(F32), rows[1][...].astype(F32)]
    e.append(low_rows[pl.ds(pl.multiple_of(64 + 8 * y, 8), 8)])
    for n in (4, 2):
        e.append([low_rows[pl.ds(8 * n + n * y + i, 1)] for i in range(n)])
    levels = up_levels(c, e)
    d8, d7, d6, d5, d4, d3 = levels
    own_out[0:128] = d6
    own_out[128:384] = d7
    own_out[384:896] = d8
    last = [d6[80:128], d7[208:256], d8[464:512]]
    nodes = [d3, d4, d5, d6[0:48], d7[0:48], d8[0:48]] + last + [jnp.zeros((16, 128), BF16)]
    packed = pack(jnp.concatenate(nodes, 0).astype(F32))
    b = tops[0].astype(F32)
    taps = jnp.zeros((8, 1024), F32)
    for f in range(FAR):
        tap = index[0, f] - node + REACH
        tap = jnp.where((f < count[0]) & (node > 0), tap, -1)
        taps = taps + jnp.where(iota((8, 1024), 0, 1) == tap, b[f : f + 1], 0.0)
    taps = [taps[:, 128 * m : 128 * m + 128] for m in range(8)]
    msg = jnp.concatenate(taps + [packed, jnp.zeros((8, 128), F32)], 0).astype(BF16)
    for p in range(8):
        msg_out[MSG * p : MSG * p + MSG] = msg


def top_kernel(ready, arrived, own, rows, out, table):
    pick, gather = pick_matrix(), gather_matrix()
    y, low = position()
    depth = sum((low >= (1 << d)).astype(jnp.int32) for d in range(1, 6))
    start, first = jnp.int32(STARTS[0]), jnp.int32(0)
    for d in range(6):
        start = jnp.where(depth == d, STARTS[d], start)
        first = jnp.where((depth == d) & (low > 0), 1 << d, first)
    planes = (0, 1, 2 + y // 4, 4 + y // 2)
    places = (start + low - first, STARTS[6] + low % 8, STARTS[7] + low % 16, STARTS[8] + low % 32)
    table[...] = jnp.zeros((NODES * 16, 128), F32)
    ready()

    def put(depth, place, value):
        s = (STARTS[depth] + place) * 16
        table[s : s + value.shape[0]] = value

    d3 = []
    for p in range(8):
        c = unpack(arrived[MSG * p + 64 : MSG * p + 96], pick)
        d3.append(c[0:16])
        put(4, REACH + 2 * p, c[16:48])
        put(5, REACH + 4 * p, c[48:112])
    c = jnp.concatenate(d3, 0)
    put(3, REACH, c)
    c = c.astype(BF16)
    e = rows[0][...].astype(F32)
    for d, c in zip((2, 1, 0), up_levels(c, [e[8:16], e[4:8], e[2:4]])):
        put(d, REACH, c.astype(F32))
    prior = unpack(arrived[pl.ds(pl.multiple_of(jnp.maximum(y - 1, 0) * MSG, 16), MSG)][88:168], pick)
    later = unpack(arrived[pl.ds(pl.multiple_of(jnp.minimum(y + 1, 7) * MSG, 16), MSG)][88:168], pick)
    mine = own[...].astype(F32)
    for i, n in enumerate((8, 16, 32)):
        put(6 + i, REACH + n, later[16 * (1 + 3 * i) : 16 * (4 + 3 * i)])
        put(6 + i, 0, prior[16 * (10 + 3 * i) : 16 * (13 + 3 * i)])
        begin = 16 * (n - 8)
        put(6 + i, REACH, mine[begin : begin + 16 * n])
    sums = []
    for s in range(4):
        taps = arrived[pl.ds(pl.multiple_of(planes[s] * MSG, 16), MSG)][0:64].astype(F32)
        acc = [None] * 8
        for o in range(TAPS):
            c = table[pl.ds(pl.multiple_of((places[s] + o) * 16, 16), 16)]
            for m in range(8):
                t = taps[8 * m + o : 8 * m + o + 1] * c
                acc[m] = t if o == 0 else acc[m] + t
        sums.append(jnp.concatenate(acc, 1))
    z = dot(jnp.concatenate(sums, 0).astype(BF16), gather)
    z = pack(z).astype(BF16)
    for i in range(64):
        out[16 * i : 16 * i + 16] = z


def side_kernel(
    ready,
    far_index,
    far_count,
    near_index,
    near_count,
    before,
    stack,
    after,
    points,
    coupling,
    block,
    zl_out,
    near_out,
    table,
    prod,
    leaves,
    halves,
):
    pick, gather, pair = pick_matrix(), gather_matrix(), pair_matrix()
    y, low = position()
    prior = y * 64 + low - 1
    prod[1008:1024] = jnp.zeros((16, 1024), BF16)
    ready()

    window = [before[256:512]]
    window += [points[:, 128 * i : 128 * i + 128] for i in range(16)]
    window += [after[256:512]]
    w = jnp.concatenate(window, 0).astype(F32)
    turned = jnp.concatenate([w[:, 64:128], w[:, 0:64]], 1)
    left = lanes((768, 128), 64) == 0
    four = [
        jnp.where(left, w, 0.0),
        jnp.where(left, 0.0, turned),
        jnp.where(left, turned, 0.0),
        jnp.where(left, 0.0, w),
    ]
    four = jnp.concatenate([x.reshape(48, 1, 16, 128) for x in four], 1)
    leaves[0:3072] = four.reshape(3072, 128).astype(BF16)
    leaves[3072:3104] = jnp.zeros((32, 128), BF16)
    slot = lanes((32, 128), 1) % NEAR

    def leaf(t):
        b = block[t].astype(F32)
        mat = jnp.concatenate([b[:, 128 * m : 128 * m + 128] for m in range(32)], 0)
        vec = []
        for f in range(NEAR):
            at = near_index[t, f] - prior * LPD
            at = jnp.where(f < near_count[t], at, 3 * LPD) * 32
            vec.append(leaves[pl.ds(pl.multiple_of(at, 32), 32)])
        r = lax.dot_general(
            jnp.concatenate(vec, 0),
            mat.astype(BF16),
            (((1,), (1,)), ((), ())),
            preferred_element_type=F32,
        )
        q = jnp.where(slot == 0, r[0:32], 0.0)
        for f in range(1, NEAR):
            q = jnp.where(slot == f, r[32 * f : 32 * f + 32], q)
        q = q.astype(BF16)
        at = pl.ds(pl.multiple_of(t * 16, 16), 16)
        halves[at, 0:128] = q[0:16]
        halves[at, 128:256] = q[16:32]

    pl.loop(0, LPD, unroll=4)(leaf)
    r = dot(halves[...], pair)
    g = lanes((16, 128), 64)
    for i in range(16):
        near_out[:, 128 * i : 128 * i + 128] = jnp.where(
            g == 0, r[32 * i : 32 * i + 16], r[32 * i + 16 : 32 * i + 32]
        )

    table[0:1024] = unpack(before[0:256], pick)
    table[1024:2048] = stack[...].astype(F32)
    table[2048:3072] = unpack(after[0:256], pick)

    def level(h):
        n = LPD >> h

        def step(t):
            b = coupling[t].astype(F32)
            acc = [None] * 8
            for f in range(FAR):
                at = far_index[t, f] - prior * n
                at = at + OFFS[h] + (64 - n) * (
                    (at >= n).astype(jnp.int32) + (at >= 2 * n).astype(jnp.int32)
                )
                at = jnp.where(f < far_count[t], at, 127) * 16
                c = table[pl.ds(pl.multiple_of(at, 16), 16)]
                for m in range(8):
                    r = b[f : f + 1, 128 * m : 128 * m + 128] * c
                    acc[m] = r if f == 0 else acc[m] + r
            prod[pl.ds(pl.multiple_of(t * 16, 16), 16)] = jnp.concatenate(acc, 1).astype(BF16)

        pl.loop(OFFS[h], OFFS[h] + n, unroll=min(n, 4))(step)

    for h in range(LEVELS):
        level(h)
    zl_out[...] = dot(prod[...], gather).astype(BF16)


def down_kernel(ready, arrived, rows, zl, transfer, basis, near, out, low_rows):
    pick, gather = pick_matrix(), gather_matrix()
    y, low = position()
    node = 512 + y * 64 + low
    ready()
    got = []
    for d in range(9):
        at = jnp.right_shift(node, 9 - d) % 64
        got.append(arrived[pl.ds(pl.multiple_of(at * 16, 16), 16)])
    first = [unpack(got[d][0:8], pick) for d in range(7)]
    second = [unpack(got[d][8:16], pick) for d in (7, 8)]
    z = [first[d][0:16] for d in range(6)]
    z += [first[6][16:32], second[0][0:16], second[1][16:32]]
    zloc = zl[...].astype(F32)
    z.append(zloc[992:1008])
    for i in range(4):
        start = 0 if i == 0 else 112 + 16 * i
        low_rows[start : start + rows[i].shape[0]] = rows[i][...].astype(F32)
    e = []
    for d in range(1, 10):
        at = jnp.right_shift(node, 9 - d)
        e.append(low_rows[pl.ds(at if d < 7 else 16 * d + at % 16 + 16, 1)])

    def spread_down(y, row):
        return jnp.concatenate([y * row[:, 128 * m : 128 * m + 128] for m in range(8)], 1)

    y = z[0]
    for d in range(1, 10):
        t = spread_down(y, e[d - 1]).astype(BF16)
        y = (dot(t, gather) + z[d]).astype(BF16).astype(F32)
    e = transfer[...].astype(F32)
    for h in range(LEVELS - 2, -1, -1):
        n = LPD >> h
        t = [
            spread_down(y[16 * (j // 2) : 16 * (j // 2) + 16], e[OFFS[h] + j : OFFS[h] + j + 1])
            for j in range(n)
        ]
        t = jnp.concatenate(t, 0).astype(BF16)
        zs = zloc[16 * OFFS[h] : 16 * (OFFS[h] + n)]
        y = (dot(t, gather) + zs).astype(BF16).astype(F32)
    bas = basis[...].astype(F32)
    g = lanes((16, 128), 32)
    for i in range(8):
        t = y[64 * i : 64 * i + 16]
        for k in range(1, 4):
            t = jnp.where(g == k, y[64 * i + 16 * k : 64 * i + 16 * k + 16], t)
        s = slice(256 * i, 256 * i + 256)
        far = dot(t.astype(BF16), block_basis(bas, i).astype(BF16))
        out[:, s] = (far + near[:, s]).astype(BF16)


def call(body, out, out_kinds, scratch, kinds, args, micros, parts=()):
    spaces = {"s": pltpu.SMEM, "v": pltpu.VMEM, "h": pltpu.HBM, "p": pltpu.HBM, "d": pltpu.HBM}
    held = []
    for a, k in zip(args, kinds):
        if k == "h":
            held.append(a)
        elif k == "p":
            held += [jax.ShapeDtypeStruct((rows, a.shape[1]), a.dtype) for _, rows in parts]
    sent = [o for o, k in zip(out, out_kinds) if k == "h"]

    def kernel(*refs):
        ins, outs = refs[: len(args)], refs[len(args) : len(args) + len(out)]
        rest = list(refs[len(args) + len(out) :])
        own, rest = rest[: len(scratch)], rest[len(scratch) :]
        sems = rest.pop()
        copies, given, back = [], [], []
        for r, k in zip(ins, kinds):
            if k == "h":
                v = rest.pop(0)
                copies.append(pltpu.make_async_copy(r, v, sems.at[len(copies)]))
                given.append(v)
            elif k == "p":
                blocks = []
                for first, rows in parts:
                    v = rest.pop(0)
                    at = first(*position()) if callable(first) else first
                    at = pl.multiple_of(at, 16) if callable(first) else at
                    src = r.at[pl.ds(at, rows)]
                    copies.append(pltpu.make_async_copy(src, v, sems.at[len(copies)]))
                    blocks.append(v)
                given.append(blocks)
            elif k != "d":
                given.append(r)
        for r, k in zip(outs, out_kinds):
            if k == "h":
                v = rest.pop(0)
                back.append(pltpu.make_async_copy(v, r, sems.at[len(copies) + len(back)]))
                given.append(v)
            else:
                given.append(r)
        for c in copies:
            c.start()

        def ready():
            for c in copies:
                c.wait()

        body(ready, *given, *own)
        for c in back:
            c.start()
        for c in back:
            c.wait()

    buffers = [pltpu.VMEM(a.shape, a.dtype) for a in held + sent]
    return pl.pallas_call(
        kernel,
        out_shape=out,
        in_specs=[pl.BlockSpec(memory_space=spaces[k]) for k in kinds],
        out_specs=[pl.BlockSpec(memory_space=spaces[k]) for k in out_kinds],
        scratch_shapes=list(scratch) + buffers + [pltpu.SemaphoreType.DMA((16,))],
        compiler_params=pltpu.CompilerParams(vmem_limit_bytes=VMEM_LIMIT),
        cost_estimate=pl.CostEstimate(
            flops=int(micros * 1e12), bytes_accessed=int(micros * 3.5e6), transcendentals=0
        ),
    )(*args)


def shape(rows, cols, dtype=BF16):
    return jax.ShapeDtypeStruct((rows, cols), dtype)


def local(
    points,
    basis,
    transfer,
    top_transfer,
    coupling,
    far_index,
    far_count,
    top_coupling,
    top_index,
    top_count,
    near_block,
    near_index,
    near_count,
):
    devices = 512

    root_msg, stack = call(
        up_kernel,
        [shape(512, 128), shape(1024, 128)],
        "hh",
        [],
        "hhh",
        (points, basis, transfer),
        COST[0],
    )
    plane_roots = lax.all_to_all(root_msg, PLANE, 0, 0, tiled=True)
    (ex,) = call(exchange_kernel, [shape(512, 128)], "h", [], "hh", (stack, points), COST[1])
    before = lax.ppermute(ex, ALL, [(i, i + 1) for i in range(devices - 1)])
    after = lax.ppermute(ex, ALL, [(i + 1, i) for i in range(devices - 1)])

    msg, own = call(
        plane_kernel,
        [shape(8 * MSG, 128), shape(896, 128)],
        "hh",
        [pltpu.VMEM((128, 1024), F32)],
        "sshphd",
        (top_index, top_count, plane_roots, top_transfer, top_coupling, ex),
        COST[2],
        parts=[
            (0, 128),
            (lambda y, low: 128 + 16 * y, 16),
            (lambda y, low: 256 + 32 * y, 32),
            (lambda y, low: 512 + 64 * y, 64),
        ],
    )
    planes = lax.all_to_all(msg, "y", 0, 0, tiled=True)

    (z_msg,) = call(
        top_kernel,
        [shape(1024, 128)],
        "h",
        [pltpu.VMEM((NODES * 16, 128), F32)],
        "hhp",
        (planes, own, top_transfer),
        COST[3],
        parts=[(0, 16)],
    )
    z_all = lax.all_to_all(z_msg, PLANE, 0, 0, tiled=True)
    zl, near = call(
        side_kernel,
        [shape(1024, 128), shape(VEC, LPD * LEAF, F32)],
        "hh",
        [
            pltpu.VMEM((3072, 128), F32),
            pltpu.VMEM((1024, 1024), BF16),
            pltpu.VMEM((3104, 128), BF16),
            pltpu.VMEM((512, 256), BF16),
        ],
        "sssshhhhhh",
        (
            far_index,
            far_count,
            near_index,
            near_count,
            before,
            stack,
            after,
            points,
            coupling,
            near_block,
        ),
        COST[4],
    )
    (result,) = call(
        down_kernel,
        [shape(VEC, LPD * LEAF)],
        "h",
        [pltpu.VMEM((176, 1024), F32)],
        "hphhhh",
        (z_all, top_transfer, zl, transfer, basis, near),
        COST[6],
        parts=[
            (0, 128),
            (lambda y, low: 128 + (y * 64 + low) // 4 // 16 * 16, 16),
            (lambda y, low: 256 + (y * 64 + low) // 2 // 16 * 16, 16),
            (lambda y, low: 512 + (y * 64 + low) // 16 * 16, 16),
        ],
    )
    return result


def solution(mesh):
    grid = Mesh(mesh.devices.reshape(8, 8, 2, 4), ALL)
    one, two, three = P(ALL), P(ALL, None), P(ALL, None, None)
    wide = P(None, ALL)
    placed = (wide, wide, two, P(), three, two, one, three, two, one, three, two, one)
    return jax.shard_map(local, mesh=grid, in_specs=placed, out_specs=wide, check_vma=False)
```

time: 92.6 us -> 81.8 us (0.88)
  local copies, waits for them, and re-layouts: 13.5 us -> 2.16 us
  Pallas kernels: 22.9 us -> 26.8 us
  starting transfers between devices: 39.3 us -> 36.3 us
  between operations: 1.85 us -> 0.75 us
  waiting for transfers between devices: 14.1 us -> 15.1 us
    unnamed x61 -> x8, local copies, waits for them, and re-layouts: 8.26 us -> 2.16 us
    all_to_all x1, waiting for transfers between devices: 8.77 us -> 3.96 us  [local(): planes = lax.all_to_all(msg, 'y', 0, 0, tiled=True)]
    pallas_call x6, Pallas kernels: 22.9 us -> 26.8 us  [call(): pl.pallas_call(kernel, out_shape=out, in_specs=[pl.BlockSpec(memory_space...]
    all_to_all x1, waiting for transfers between devices: 0.01 us -> 3.76 us  [local(): z_all = lax.all_to_all(z_msg, PLANE, 0, 0, tiled=True)]
    slice x3 -> x0, local copies, waits for them, and re-layouts: 2.62 us -> none  [the longest x1 0.97 us: local(): top_rows[0:126]]
    all_to_all x1, waiting for transfers between devices: 5.3 us -> 7.41 us  [local(): plane_roots = lax.all_to_all(root_msg, PLANE, 0, 0, tiled=True)]
    ppermute x1, starting transfers between devices: 5.91 us -> 4.18 us  [local(): after = lax.ppermute(ex, ALL, [(i + 1, i) for i in range(devices - 1)])]
    gather x1 -> x0, local copies, waits for them, and re-layouts: 1.66 us -> none  [local(): top_rows = top_transfer[jnp.concatenate([i.astype(jnp.int32) for i in ids])]]
  transfers between devices with their start and end apart: 5 -> 5, of which waited for: 2 -> 3; matrix products, arithmetic and copies ran while one was open for 6% -> 2% of each run, Pallas kernels for 18% -> 17%
where the time goes in v2:
time: 81.8 us; the launch traced here: 81.1 us
  starting transfers between devices  36.3 us (44%)
  Pallas kernels  26.8 us (33%)
  waiting for transfers between devices  15.1 us (18%)
  local copies, waits for them, and re-layouts  2.16 us (3%)
    pallas_call x6, Pallas kernels, call(): pl.pallas_call(kernel, out_shape=out, in_specs=[pl.BlockSpec(memory_space...  26.8 us
    all_to_all x1, starting transfers between devices, local(): plane_roots = lax.all_to_all(root_msg, PLANE, 0, 0, tiled=True)  15 us
    all_to_all x1, starting transfers between devices, local(): z_all = lax.all_to_all(z_msg, PLANE, 0, 0, tiled=True)  8.3 us
    all_to_all x1, waiting for transfers between devices, local(): plane_roots = lax.all_to_all(root_msg, PLANE, 0, 0, tiled=True)  7.41 us
    all_to_all x1, starting transfers between devices, local(): planes = lax.all_to_all(msg, 'y', 0, 0, tiled=True)  6.83 us
    ppermute x1, starting transfers between devices, local(): after = lax.ppermute(ex, ALL, [(i + 1, i) for i in range(devices - 1)])  4.18 us
    all_to_all x1, waiting for transfers between devices, local(): planes = lax.all_to_all(msg, 'y', 0, 0, tiled=True)  3.96 us
    all_to_all x1, waiting for transfers between devices, local(): z_all = lax.all_to_all(z_msg, PLANE, 0, 0, tiled=True)  3.76 us
  transfers between devices with their start and end apart: 5, of which 3 were waited for; matrix products, arithmetic and copies ran while one was open for 2% of the time, Pallas kernels for 17%

profile of v2, /device:TPU:1, one launch (start us, length us, event | category | flops | bytes accessed | tf_op | source)
XLA Modules:
  0.0 81.1 jit_solution(18037733790687696674)
XLA Ops:
  0.0 3.5 %shard_map.127 = (bf16[512,128]{1,0:T(8,128)(2,1)}, bf16[1024,128]{1,0:T(8,128)(2,1)}) custom-call(bf16[16,2048]{1,0:T(8,128)(2,1)} %refs_7_.1, bf16[32,2048]{1,0:T(8,128)(2,1)} %refs_4_.3, bf16[62,1024]{1,0:T(8,128)(2,1)} %refs_3_.5), custom_call_target="tpu_custom_call" | custom-call | flops 3999999983616 | bytes 14000000 | tf_op jit(solution)/shard_map/pallas_call | solution.py:457
  3.5 15.0 %all-to-all-start = ((bf16[64,8,128]{2,1,0:T(8,128)(2,1)}), bf16[64,8,128]{2,1,0:T(8,128)(2,1)}, u32[]{:S(2)}, u32[]{:S(2)}) async-start(bf16[64,8,128]{2,1,0:T(8,128)(2,1)} %bitcast.9), calls=%async_computation | async-start | bytes 262144 | tf_op jit(solution)/shard_map/all_to_all | solution.py:500
  18.5 1.8 %shard_map.128.refs_5_ = bf16[512,128]{1,0:T(8,128)(2,1)} custom-call(bf16[1024,128]{1,0:T(8,128)(2,1)} %get-tuple-element.12.refs_0_.refs_5_, bf16[16,2048]{1,0:T(8,128)(2,1)} %refs_7_.1), custom_call_target="tpu_custom_call" | custom-call | flops 999999995904 | bytes 3500000 | tf_op jit(solution)/shard_map/pallas_call | solution.py:457
  21.0 7.4 %all-to-all-done = bf16[64,8,128]{2,1,0:T(8,128)(2,1)} async-done(((bf16[64,8,128]{2,1,0:T(8,128)(2,1)}), bf16[64,8,128]{2,1,0:T(8,128)(2,1)}, u32[]{:S(2)}, u32[]{:S(2)}) %all-to-all-start) | async-done | bytes 131104 | tf_op jit(solution)/shard_map/all_to_all | solution.py:500
  28.4 0.0 copy-start.1
  28.4 0.0 copy-start.2
  28.4 5.0 %shard_map.129 = (bf16[1408,128]{1,0:T(8,128)(2,1)}, bf16[896,128]{1,0:T(8,128)(2,1)}) custom-call(s32[1,4]{1,0:T(1,128)} %refs_0_.4, s32[1]{0:T(128)S(6)} %copy.16.refs_1_, bf16[512,128]{1,0:T(8,128)(2,1)} %bitcast.1.refs_2_, bf16[1024,1024]{1,0:T(8,128)(2,1)} %refs_1_.8, bf16[1,4,1024]{2,1,0:T(4,128)(2,1)} %refs_4_.2, bf16[512,128]{1,0:T(8,128)(2,1)} %shard_map.128.refs_5_), custom_call_target="tpu_custom_call" | custom-call | flops 3999999983616 | bytes 14000000 | tf_op jit(solution)/shard_map/pallas_call | solution.py:457
  33.4 6.8 %all-to-all-start.1 = ((bf16[8,176,128]{2,1,0:T(8,128)(2,1)}), bf16[8,176,128]{2,1,0:T(8,128)(2,1)S(1)}, u32[]{:S(2)}, u32[]{:S(2)}) async-start(bf16[8,176,128]{2,1,0:T(8,128)(2,1)} %bitcast.7), calls=%async_computation.1 | async-start | bytes 720896 | tf_op jit(solution)/shard_map/all_to_all | solution.py:520
  40.2 4.2 %collective-permute-start.1 = (bf16[512,128]{1,0:T(8,128)(2,1)}, bf16[512,128]{1,0:T(8,128)(2,1)}, u32[]{:S(2)}, u32[]{:S(2)}) collective-permute-start(bf16[512,128]{1,0:T(8,128)(2,1)} %shard_map.128.refs_5_), channel_id=1, source_target_pairs={{1,0},{2,1},{3,2},{4,3},{5,4},{6,5},{7,6},{8,7},{9,8},{10,9},{11,1... | collective-permute-start | bytes 393224 | tf_op jit(solution)/shard_map/ppermute | solution.py:503
  44.4 1.9 %collective-permute-start = (bf16[512,128]{1,0:T(8,128)(2,1)}, bf16[512,128]{1,0:T(8,128)(2,1)}, u32[]{:S(2)}, u32[]{:S(2)}) collective-permute-start(bf16[512,128]{1,0:T(8,128)(2,1)} %shard_map.128.refs_5_), channel_id=1, source_target_pairs={{0,1},{1,2},{2,3},{3,4},{4,5},{5,6},{6,7},{7,8},{8,9},{9,10},{10,1... | collective-permute-start | bytes 393224 | tf_op jit(solution)/shard_map/ppermute | solution.py:502
  46.4 0.0 copy-done.1
  46.4 0.7 copy.15.refs_2_
  47.0 0.0 copy-done.2
  47.0 0.7 copy.14.refs_0_
  47.8 4.0 %all-to-all-done.1 = bf16[8,176,128]{2,1,0:T(8,128)(2,1)S(1)} async-done(((bf16[8,176,128]{2,1,0:T(8,128)(2,1)}), bf16[8,176,128]{2,1,0:T(8,128)(2,1)S(1)}, u32[]{:S(2)}, u32[]{:S(2)}) %all-to-all-start.1) | async-done | bytes 360480 | tf_op jit(solution)/shard_map/all_to_all | solution.py:520
  51.7 0.0 copy-start
  51.7 0.7 copy-done
  52.5 3.1 %shard_map.130 = bf16[1024,128]{1,0:T(8,128)(2,1)} custom-call(bf16[1408,128]{1,0:T(8,128)(2,1)} %bitcast.6, bf16[896,128]{1,0:T(8,128)(2,1)} %get-tuple-element.14.refs_1_, bf16[1024,1024]{1,0:T(8,128)(2,1)} %refs_1_.8), custom_call_target="tpu_custom_call" | custom-call | flops 3000000053248 | bytes 10500000 | tf_op jit(solution)/shard_map/pallas_call | solution.py:457
  55.6 8.3 %all-to-all-start.2 = ((bf16[64,16,128]{2,1,0:T(8,128)(2,1)}), bf16[64,16,128]{2,1,0:T(8,128)(2,1)}, u32[]{:S(2)}, u32[]{:S(2)}) async-start(bf16[64,16,128]{2,1,0:T(8,128)(2,1)} %bitcast.8), calls=%async_computation.2 | async-start | bytes 524288 | tf_op jit(solution)/shard_map/all_to_all | solution.py:532
  63.9 0.0 collective-permute-done.1.refs_6_
  63.9 0.0 collective-permute-done.refs_4_
  63.9 8.6 %shard_map.131 = (bf16[1024,128]{1,0:T(8,128)(2,1)}, f32[16,2048]{1,0:T(8,128)}) custom-call(s32[63,4]{1,0:T(8,128)} %copy.14.refs_0_, s32[63]{0:T(128)} %refs_1_.7, s32[32,4]{1,0:T(8,128)} %copy.15.refs_2_, s32[32]{0:T(128)} %refs_3_.4, bf16[512,128]{1,0:T(8,128)(2,1)} %collective-permute-done.refs_4_, bf16[1024,128]{1,0:T(8,128)(2,1)} %get-tuple-element.12.refs_0_.refs_5_, ...), custom_call_target="tpu_custom_call" | custom-call | flops 7999999967232 | bytes 28000000 | tf_op jit(solution)/shard_map/pallas_call | solution.py:457
  72.5 3.8 %all-to-all-done.2 = bf16[64,16,128]{2,1,0:T(8,128)(2,1)} async-done(((bf16[64,16,128]{2,1,0:T(8,128)(2,1)}), bf16[64,16,128]{2,1,0:T(8,128)(2,1)}, u32[]{:S(2)}, u32[]{:S(2)}) %all-to-all-start.2) | async-done | bytes 262176 | tf_op jit(solution)/shard_map/all_to_all | solution.py:532
  76.3 4.9 %shard_map.132 = bf16[16,2048]{1,0:T(8,128)(2,1)} custom-call(bf16[1024,128]{1,0:T(8,128)(2,1)} %bitcast.5.refs_0_, bf16[1024,1024]{1,0:T(8,128)(2,1)} %refs_1_.8, bf16[1024,128]{1,0:T(8,128)(2,1)} %get-tuple-element.15.refs_2_, bf16[62,1024]{1,0:T(8,128)(2,1)} %refs_3_.5, bf16[32,2048]{1,0:T(8,128)(2,1)} %refs_4_.3, f32[16,2048]{1,0:T(8,128)} %get-tuple-element.16.refs_5_), custom_call_target="tpu_custom_call" | custom-call | flops 3999999983616 | bytes 14000000 | tf_op jit(solution)/shard_map/pallas_call | solution.py:457
Async XLA Ops:
  3.5 24.9 %all-to-all-start = ((bf16[64,8,128]{2,1,0:T(8,128)(2,1)}), bf16[64,8,128]{2,1,0:T(8,128)(2,1)}, u32[]{:S(2)}, u32[]{:S(2)}) async-start(bf16[64,8,128]{2,1,0:T(8,128)(2,1)} %bitcast.9), calls=%async_computation | async-start | bytes 262144 | tf_op jit(solution)/shard_map/all_to_all | solution.py:500
  28.4 18.0 %copy-start.1 = (s32[32,4]{0,1:T(4,128)S(1)}, s32[32,4]{0,1:T(4,128)}, u32[]{:S(2)}) copy-start(s32[32,4]{0,1:T(4,128)} %param.24) | copy-start | bytes 1540
  28.4 18.7 %copy-start.2 = (s32[63,4]{0,1:T(4,128)S(1)}, s32[63,4]{0,1:T(4,128)}, u32[]{:S(2)}) copy-start(s32[63,4]{0,1:T(4,128)} %param.18) | copy-start | bytes 3028
  33.4 18.3 %all-to-all-start.1 = ((bf16[8,176,128]{2,1,0:T(8,128)(2,1)}), bf16[8,176,128]{2,1,0:T(8,128)(2,1)S(1)}, u32[]{:S(2)}, u32[]{:S(2)}) async-start(bf16[8,176,128]{2,1,0:T(8,128)(2,1)} %bitcast.7), calls=%async_computation.1 | async-start | bytes 720896 | tf_op jit(solution)/shard_map/all_to_all | solution.py:520
  40.2 23.7 %collective-permute-start.1 = (bf16[512,128]{1,0:T(8,128)(2,1)}, bf16[512,128]{1,0:T(8,128)(2,1)}, u32[]{:S(2)}, u32[]{:S(2)}) collective-permute-start(bf16[512,128]{1,0:T(8,128)(2,1)} %shard_map.128.refs_5_), channel_id=1, source_target_pairs={{1,0},{2,1},{3,2},{4,3},{5,4},{6,5},{7,6},{8,7},{9,8},{10,9},{11,1... | collective-permute-start | bytes 393224 | tf_op jit(solution)/shard_map/ppermute | solution.py:503
  44.4 19.5 %collective-permute-start = (bf16[512,128]{1,0:T(8,128)(2,1)}, bf16[512,128]{1,0:T(8,128)(2,1)}, u32[]{:S(2)}, u32[]{:S(2)}) collective-permute-start(bf16[512,128]{1,0:T(8,128)(2,1)} %shard_map.128.refs_5_), channel_id=1, source_target_pairs={{0,1},{1,2},{2,3},{3,4},{4,5},{5,6},{6,7},{7,8},{8,9},{9,10},{10,1... | collective-permute-start | bytes 393224 | tf_op jit(solution)/shard_map/ppermute | solution.py:502
  51.7 0.7 copy-start
  55.6 20.7 %all-to-all-start.2 = ((bf16[64,16,128]{2,1,0:T(8,128)(2,1)}), bf16[64,16,128]{2,1,0:T(8,128)(2,1)}, u32[]{:S(2)}, u32[]{:S(2)}) async-start(bf16[64,16,128]{2,1,0:T(8,128)(2,1)} %bitcast.8), calls=%async_computation.2 | async-start | bytes 524288 | tf_op jit(solution)/shard_map/all_to_all | solution.py:532

commit v3 on v2

--- a/solution.py
+++ b/solution.py
@@ -19,11 +19,11 @@
 PLANE = ("z", "core", "x")
 REACH = 3
 TAPS = 2 * REACH + 1
-MSG = 176
+MSG = 128
 SIZES = [(1 << d) + 2 * REACH for d in range(6)] + [8 + 6, 16 + 6, 32 + 6]
 STARTS = [sum(SIZES[:d]) for d in range(9)]
 NODES = sum(SIZES)
-VMEM_LIMIT = 56 << 20
+VMEM_LIMIT = 32 << 20
 COST = (4, 1, 4, 3, 8, 4, 4)
 F32 = jnp.float32
 BF16 = jnp.bfloat16
@@ -153,14 +153,35 @@
     stack_out[...] = jnp.concatenate(levels + [jnp.zeros((16, 128), BF16)], 0)
 
 
-def exchange_kernel(ready, stack, points, ex_out):
+def exchange_kernel(ready, stack, points, ex_out, chain_out, rows, low_rows):
     ready()
     ex_out[0:256] = pack(stack[...].astype(F32)).astype(BF16)
     for i in range(16):
         ex_out[256 + 16 * i : 272 + 16 * i] = points[:, 128 * i : 128 * i + 128]
-
-
-def plane_kernel(ready, index, count, arrived, rows, tops, msg_out, own_out, low_rows):
+    y, low = position()
+    node = 512 + y * 64 + low
+    one, rest, fold = spread_matrix(False), spread_matrix(True), fold_matrix()
+    q = mask(iota((32, 128), 0, 1) == iota((32, 128), 1, 1))
+    for c in ready.rest:
+        c.wait()
+    ready.rest.clear()
+    low_rows[0:128] = rows[0:128].astype(F32)
+    low_rows[128:176] = rows[240:288].astype(F32)
+    for d in range(9, 0, -1):
+        at = jnp.right_shift(node, 9 - d)
+        t = dot(q, one if d == 9 else rest)
+        t = t * low_rows[pl.ds(at if d < 7 else 16 * d + at % 16 + 16, 1)]
+        p = t[:, 0:128]
+        for m in range(1, 8):
+            p = p + t[:, 128 * m : 128 * m + 128]
+        q = p.astype(BF16)
+        g = dot(q, fold).astype(BF16)
+        chain_out[:, 128 * (d - 1) : 128 * d] = jnp.concatenate([g] * 4, 0)
+
+
+def plane_kernel(
+    ready, index, count, arrived, rows, tops, msg_out, own_out, low_rows
+):
     pick = pick_matrix()
     y, low = position()
     node = y * 64 + low
@@ -170,8 +191,8 @@
         [w[:, 0:128].reshape(64, 1, 8, 128), w[:, 128:256].reshape(64, 1, 8, 128)], 1
     )
     c = c.reshape(1024, 128).astype(BF16)
-    low_rows[...] = rows[0][...].astype(F32)
-    e = [rows[3][...].astype(F32), rows[2][...].astype(F32), rows[1][...].astype(F32)]
+    low_rows[...] = rows[0:128].astype(F32)
+    e = [rows[176:240].astype(F32), rows[144:176].astype(F32), rows[128:144].astype(F32)]
     e.append(low_rows[pl.ds(pl.multiple_of(64 + 8 * y, 8), 8)])
     for n in (4, 2):
         e.append([low_rows[pl.ds(8 * n + n * y + i, 1)] for i in range(n)])
@@ -180,9 +201,9 @@
     own_out[0:128] = d6
     own_out[128:384] = d7
     own_out[384:896] = d8
-    last = [d6[80:128], d7[208:256], d8[464:512]]
-    nodes = [d3, d4, d5, d6[0:48], d7[0:48], d8[0:48]] + last + [jnp.zeros((16, 128), BF16)]
-    packed = pack(jnp.concatenate(nodes, 0).astype(F32))
+    inner = [d3, d4, d5]
+    first = pack(jnp.concatenate(inner + [d6[0:48], d7[0:48], d8[0:48]], 0).astype(F32))
+    last = pack(jnp.concatenate(inner + [d6[80:128], d7[208:256], d8[464:512]], 0).astype(F32))
     b = tops[0].astype(F32)
     taps = jnp.zeros((8, 1024), F32)
     for f in range(FAR):
@@ -190,9 +211,10 @@
         tap = jnp.where((f < count[0]) & (node > 0), tap, -1)
         taps = taps + jnp.where(iota((8, 1024), 0, 1) == tap, b[f : f + 1], 0.0)
     taps = [taps[:, 128 * m : 128 * m + 128] for m in range(8)]
-    msg = jnp.concatenate(taps + [packed, jnp.zeros((8, 128), F32)], 0).astype(BF16)
+    taps = jnp.concatenate(taps, 0).astype(BF16)
     for p in range(8):
-        msg_out[MSG * p : MSG * p + MSG] = msg
+        msg_out[MSG * p : MSG * p + 64] = taps
+        msg_out[MSG * p + 64 : MSG * p + 128] = jnp.where(y < p, last, first).astype(BF16)
 
 
 def top_kernel(ready, arrived, own, rows, out, table):
@@ -221,15 +243,15 @@
     c = jnp.concatenate(d3, 0)
     put(3, REACH, c)
     c = c.astype(BF16)
-    e = rows[0][...].astype(F32)
+    e = rows[...].astype(F32)
     for d, c in zip((2, 1, 0), up_levels(c, [e[8:16], e[4:8], e[2:4]])):
         put(d, REACH, c.astype(F32))
-    prior = unpack(arrived[pl.ds(pl.multiple_of(jnp.maximum(y - 1, 0) * MSG, 16), MSG)][88:168], pick)
-    later = unpack(arrived[pl.ds(pl.multiple_of(jnp.minimum(y + 1, 7) * MSG, 16), MSG)][88:168], pick)
+    prior = unpack(arrived[pl.ds(pl.multiple_of(jnp.maximum(y - 1, 0) * MSG, 16), MSG)][64:128], pick)
+    later = unpack(arrived[pl.ds(pl.multiple_of(jnp.minimum(y + 1, 7) * MSG, 16), MSG)][64:128], pick)
     mine = own[...].astype(F32)
     for i, n in enumerate((8, 16, 32)):
-        put(6 + i, REACH + n, later[16 * (1 + 3 * i) : 16 * (4 + 3 * i)])
-        put(6 + i, 0, prior[16 * (10 + 3 * i) : 16 * (13 + 3 * i)])
+        put(6 + i, REACH + n, later[16 * (7 + 3 * i) : 16 * (10 + 3 * i)])
+        put(6 + i, 0, prior[16 * (7 + 3 * i) : 16 * (10 + 3 * i)])
         begin = 16 * (n - 8)
         put(6 + i, REACH, mine[begin : begin + 16 * n])
     sums = []
@@ -349,36 +371,33 @@
     zl_out[...] = dot(prod[...], gather).astype(BF16)
 
 
-def down_kernel(ready, arrived, rows, zl, transfer, basis, near, out, low_rows):
-    pick, gather = pick_matrix(), gather_matrix()
+def down_kernel(ready, arrived, chain, zl, transfer, basis, near, out):
+    gather = gather_matrix()
     y, low = position()
     node = 512 + y * 64 + low
     ready()
-    got = []
+    parts = []
+    g = lanes((8, 128), 32)
     for d in range(9):
         at = jnp.right_shift(node, 9 - d) % 64
-        got.append(arrived[pl.ds(pl.multiple_of(at * 16, 16), 16)])
-    first = [unpack(got[d][0:8], pick) for d in range(7)]
-    second = [unpack(got[d][8:16], pick) for d in (7, 8)]
-    z = [first[d][0:16] for d in range(6)]
-    z += [first[6][16:32], second[0][0:16], second[1][16:32]]
+        got = arrived[pl.ds(pl.multiple_of(at * 16, 16), 16)].astype(F32)
+        got = got[0:8] if d < 7 else got[8:16]
+        q = 2 if d in (6, 8) else 0
+        parts.append(
+            jnp.concatenate([jnp.where(g == q, got, 0.0), jnp.where(g == q + 1, got, 0.0)], 0)
+        )
+    y = lax.dot_general(
+        jnp.concatenate(parts, 1).astype(BF16),
+        chain[...],
+        (((1,), (1,)), ((), ())),
+        preferred_element_type=F32,
+    )
     zloc = zl[...].astype(F32)
-    z.append(zloc[992:1008])
-    for i in range(4):
-        start = 0 if i == 0 else 112 + 16 * i
-        low_rows[start : start + rows[i].shape[0]] = rows[i][...].astype(F32)
-    e = []
-    for d in range(1, 10):
-        at = jnp.right_shift(node, 9 - d)
-        e.append(low_rows[pl.ds(at if d < 7 else 16 * d + at % 16 + 16, 1)])
+    y = (y + zloc[992:1008]).astype(BF16).astype(F32)
 
     def spread_down(y, row):
         return jnp.concatenate([y * row[:, 128 * m : 128 * m + 128] for m in range(8)], 1)
 
-    y = z[0]
-    for d in range(1, 10):
-        t = spread_down(y, e[d - 1]).astype(BF16)
-        y = (dot(t, gather) + z[d]).astype(BF16).astype(F32)
     e = transfer[...].astype(F32)
     for h in range(LEVELS - 2, -1, -1):
         n = LPD >> h
@@ -400,14 +419,9 @@
         out[:, s] = (far + near[:, s]).astype(BF16)
 
 
-def call(body, out, out_kinds, scratch, kinds, args, micros, parts=()):
-    spaces = {"s": pltpu.SMEM, "v": pltpu.VMEM, "h": pltpu.HBM, "p": pltpu.HBM, "d": pltpu.HBM}
-    held = []
-    for a, k in zip(args, kinds):
-        if k == "h":
-            held.append(a)
-        elif k == "p":
-            held += [jax.ShapeDtypeStruct((rows, a.shape[1]), a.dtype) for _, rows in parts]
+def call(body, out, out_kinds, scratch, kinds, args, micros, direct=()):
+    spaces = {"s": pltpu.SMEM, "v": pltpu.VMEM, "w": pltpu.VMEM, "h": pltpu.HBM, "r": pltpu.HBM}
+    held = [a for a, k in zip(args, kinds) if k == "h"]
     sent = [o for o, k in zip(out, out_kinds) if k == "h"]
 
     def kernel(*refs):
@@ -415,56 +429,65 @@
         rest = list(refs[len(args) + len(out) :])
         own, rest = rest[: len(scratch)], rest[len(scratch) :]
         sems = rest.pop()
-        copies, given, back = [], [], []
+        copies, given, back, straight = [], [], [], []
         for r, k in zip(ins, kinds):
             if k == "h":
                 v = rest.pop(0)
                 copies.append(pltpu.make_async_copy(r, v, sems.at[len(copies)]))
                 given.append(v)
-            elif k == "p":
-                blocks = []
-                for first, rows in parts:
-                    v = rest.pop(0)
-                    at = first(*position()) if callable(first) else first
-                    at = pl.multiple_of(at, 16) if callable(first) else at
-                    src = r.at[pl.ds(at, rows)]
-                    copies.append(pltpu.make_async_copy(src, v, sems.at[len(copies)]))
-                    blocks.append(v)
-                given.append(blocks)
-            elif k != "d":
+            elif k != "r":
                 given.append(r)
         for r, k in zip(outs, out_kinds):
             if k == "h":
                 v = rest.pop(0)
                 back.append(pltpu.make_async_copy(v, r, sems.at[len(copies) + len(back)]))
                 given.append(v)
-            else:
+            elif k != "r":
                 given.append(r)
-        for c in copies:
+        for i, first, rows, o, to in direct:
+            src, dst = ins[i], outs[o]
+            if rows:
+                at = first(*position()) if callable(first) else first
+                at = pl.multiple_of(at, 16) if callable(first) else at
+                src, dst = src.at[pl.ds(at, rows)], dst.at[pl.ds(to, rows)]
+            sem = sems.at[len(copies) + len(back) + len(straight)]
+            straight.append(pltpu.make_async_copy(src, dst, sem))
+        for c in copies + straight:
             c.start()
 
         def ready():
             for c in copies:
                 c.wait()
 
+        ready.rest = straight
         body(ready, *given, *own)
         for c in back:
             c.start()
-        for c in back:
+        for c in back + straight:
             c.wait()
 
     buffers = [pltpu.VMEM(a.shape, a.dtype) for a in held + sent]
     return pl.pallas_call(
         kernel,
-        out_shape=out,
+        out_shape=[
+            (pltpu.HBM if k == "h" else pltpu.VMEM)(o.shape, o.dtype)
+            for o, k in zip(out, out_kinds)
+        ],
         in_specs=[pl.BlockSpec(memory_space=spaces[k]) for k in kinds],
-        out_specs=[pl.BlockSpec(memory_space=spaces[k]) for k in out_kinds],
-        scratch_shapes=list(scratch) + buffers + [pltpu.SemaphoreType.DMA((16,))],
+        out_specs=[
+            pl.BlockSpec(memory_space=pltpu.HBM if k == "h" else pltpu.VMEM) for k in out_kinds
+        ],
+        scratch_shapes=list(scratch) + buffers + [pltpu.SemaphoreType.DMA((24,))],
         compiler_params=pltpu.CompilerParams(vmem_limit_bytes=VMEM_LIMIT),
         cost_estimate=pl.CostEstimate(
             flops=int(micros * 1e12), bytes_accessed=int(micros * 3.5e6), transcendentals=0
         ),
-    )(*args)
+    )(
+        *[
+            pltpu.with_memory_space_constraint(a, spaces[k]) if k in "whr" else a
+            for a, k in zip(args, kinds)
+        ]
+    )
 
 
 def shape(rows, cols, dtype=BF16):
@@ -488,6 +511,9 @@
 ):
     devices = 512
 
+    def like(*arrays):
+        return [jax.ShapeDtypeStruct(a.shape, a.dtype) for a in arrays]
+
     root_msg, stack = call(
         up_kernel,
         [shape(512, 128), shape(1024, 128)],
@@ -498,49 +524,61 @@
         COST[0],
     )
     plane_roots = lax.all_to_all(root_msg, PLANE, 0, 0, tiled=True)
-    (ex,) = call(exchange_kernel, [shape(512, 128)], "h", [], "hh", (stack, points), COST[1])
+
+    ex, chain, rows, tops = call(
+        exchange_kernel,
+        [shape(512, 128), shape(128, 1152), shape(288, 1024)] + like(top_coupling),
+        "hhqr",
+        [pltpu.VMEM((176, 1024), F32)],
+        "hhrr",
+        (stack, points, top_transfer, top_coupling),
+        COST[1],
+        direct=[
+            (2, 0, 128, 2, 0),
+            (2, lambda y, low: 128 + (y * 64 + low) // 4 // 16 * 16, 16, 2, 240),
+            (2, lambda y, low: 256 + (y * 64 + low) // 2 // 16 * 16, 16, 2, 256),
+            (2, lambda y, low: 512 + (y * 64 + low) // 16 * 16, 16, 2, 272),
+            (2, lambda y, low: 512 + 64 * y, 64, 2, 176),
+            (2, lambda y, low: 256 + 32 * y, 32, 2, 144),
+            (2, lambda y, low: 128 + 16 * y, 16, 2, 128),
+            (3, 0, 0, 3, 0),
+        ],
+    )
     before = lax.ppermute(ex, ALL, [(i, i + 1) for i in range(devices - 1)])
     after = lax.ppermute(ex, ALL, [(i + 1, i) for i in range(devices - 1)])
 
-    msg, own = call(
+    msg, own, first_rows = call(
         plane_kernel,
-        [shape(8 * MSG, 128), shape(896, 128)],
-        "hh",
+        [shape(8 * MSG, 128), shape(896, 128), shape(16, 1024)],
+        "hvr",
         [pltpu.VMEM((128, 1024), F32)],
-        "sshphd",
-        (top_index, top_count, plane_roots, top_transfer, top_coupling, ex),
+        "sswvvr",
+        (top_index, top_count, plane_roots, rows, tops, top_transfer),
         COST[2],
-        parts=[
-            (0, 128),
-            (lambda y, low: 128 + 16 * y, 16),
-            (lambda y, low: 256 + 32 * y, 32),
-            (lambda y, low: 512 + 64 * y, 64),
-        ],
+        direct=[(5, 0, 16, 2, 0)],
     )
     planes = lax.all_to_all(msg, "y", 0, 0, tiled=True)
-
     (z_msg,) = call(
         top_kernel,
         [shape(1024, 128)],
         "h",
         [pltpu.VMEM((NODES * 16, 128), F32)],
-        "hhp",
-        (planes, own, top_transfer),
+        "wvv",
+        (planes, own, first_rows),
         COST[3],
-        parts=[(0, 16)],
     )
     z_all = lax.all_to_all(z_msg, PLANE, 0, 0, tiled=True)
-    zl, near = call(
+    zl, near, held_chain, held_transfer, held_basis = call(
         side_kernel,
-        [shape(1024, 128), shape(VEC, LPD * LEAF, F32)],
-        "hh",
+        [shape(1024, 128), shape(VEC, LPD * LEAF, F32)] + like(chain, transfer, basis),
+        "vvrrr",
         [
             pltpu.VMEM((3072, 128), F32),
             pltpu.VMEM((1024, 1024), BF16),
             pltpu.VMEM((3104, 128), BF16),
             pltpu.VMEM((512, 256), BF16),
         ],
-        "sssshhhhhh",
+        "sssswhwhhhrrr",
         (
             far_index,
             far_count,
@@ -552,23 +590,21 @@
             points,
             coupling,
             near_block,
+            chain,
+            transfer,
+            basis,
         ),
         COST[4],
+        direct=[(10, 0, 0, 2, 0), (11, 0, 0, 3, 0), (12, 0, 0, 4, 0)],
     )
     (result,) = call(
         down_kernel,
         [shape(VEC, LPD * LEAF)],
         "h",
-        [pltpu.VMEM((176, 1024), F32)],
-        "hphhhh",
-        (z_all, top_transfer, zl, transfer, basis, near),
+        [],
+        "wvvvvv",
+        (z_all, held_chain, zl, held_transfer, held_basis, near),
         COST[6],
-        parts=[
-            (0, 128),
-            (lambda y, low: 128 + (y * 64 + low) // 4 // 16 * 16, 16),
-            (lambda y, low: 256 + (y * 64 + low) // 2 // 16 * 16, 16),
-            (lambda y, low: 512 + (y * 64 + low) // 16 * 16, 16),
-        ],
     )
     return result
 

time: 81.8 us -> 75.8 us (0.927)
  Pallas kernels: 26.8 us -> 24.8 us
  local copies, waits for them, and re-layouts: 2.16 us -> 0.22 us
  waiting for transfers between devices: 15.1 us -> 13.3 us
    pallas_call x6, Pallas kernels: 26.8 us -> 24.8 us  [call(): pl.pallas_call(kernel, out_shape=[(pltpu.HBM if k == 'h' else pltpu.VMEM)...]
    unnamed x8 -> x12, local copies, waits for them, and re-layouts: 2.16 us -> 0.22 us
    all_to_all x1, waiting for transfers between devices: 7.41 us -> 5.58 us  [local(): plane_roots = lax.all_to_all(root_msg, PLANE, 0, 0, tiled=True)]
    all_to_all x1, waiting for transfers between devices: 3.96 us -> 3.05 us  [local(): planes = lax.all_to_all(msg, 'y', 0, 0, tiled=True)]
    all_to_all x1, waiting for transfers between devices: 3.76 us -> 4.63 us  [local(): z_all = lax.all_to_all(z_msg, PLANE, 0, 0, tiled=True)]
  transfers between devices with their start and end apart: 5 -> 5, of which waited for: 3 -> 3; matrix products, arithmetic and copies ran while one was open for 2% -> 0% of each run, Pallas kernels for 17% -> 18%
where the time goes in v3:
time: 75.8 us; the launch traced here: 75.3 us
  starting transfers between devices  36.3 us (48%)
  Pallas kernels  24.8 us (33%)
  waiting for transfers between devices  13.3 us (18%)
  between operations  0.77 us (1%)
    pallas_call x6, Pallas kernels, call(): pl.pallas_call(kernel, out_shape=[(pltpu.HBM if k == 'h' else pltpu.VMEM)...  24.8 us
    all_to_all x1, starting transfers between devices, local(): plane_roots = lax.all_to_all(root_msg, PLANE, 0, 0, tiled=True)  15 us
    all_to_all x1, starting transfers between devices, local(): z_all = lax.all_to_all(z_msg, PLANE, 0, 0, tiled=True)  8.31 us
    all_to_all x1, starting transfers between devices, local(): planes = lax.all_to_all(msg, 'y', 0, 0, tiled=True)  6.83 us
    all_to_all x1, waiting for transfers between devices, local(): plane_roots = lax.all_to_all(root_msg, PLANE, 0, 0, tiled=True)  5.58 us
    all_to_all x1, waiting for transfers between devices, local(): z_all = lax.all_to_all(z_msg, PLANE, 0, 0, tiled=True)  4.63 us
    ppermute x1, starting transfers between devices, local(): after = lax.ppermute(ex, ALL, [(i + 1, i) for i in range(devices - 1)])  4.18 us
    all_to_all x1, waiting for transfers between devices, local(): planes = lax.all_to_all(msg, 'y', 0, 0, tiled=True)  3.05 us
  transfers between devices with their start and end apart: 5, of which 3 were waited for; matrix products, arithmetic and copies ran while one was open for 0% of the time, Pallas kernels for 18%

profile of v3, /device:TPU:1, one launch (start us, length us, event | category | flops | bytes accessed | tf_op | source)
XLA Modules:
  0.0 75.3 jit_solution(1249603309021684683)
XLA Ops:
  0.0 3.6 %shard_map.127 = (bf16[512,128]{1,0:T(8,128)(2,1)}, bf16[1024,128]{1,0:T(8,128)(2,1)}) custom-call(bf16[16,2048]{1,0:T(8,128)(2,1)} %refs_7_.1, bf16[32,2048]{1,0:T(8,128)(2,1)} %refs_12_.1, bf16[62,1024]{1,0:T(8,128)(2,1)} %refs_11_.1), custom_call_target="tpu_custom_call" | custom-call | flops 3999999983616 | bytes 14000000 | tf_op jit(solution)/shard_map/pallas_call | solution.py:470
  3.6 15.0 %all-to-all-start = ((bf16[64,8,128]{2,1,0:T(8,128)(2,1)}), bf16[64,8,128]{2,1,0:T(8,128)(2,1)}, u32[]{:S(2)}, u32[]{:S(2)}) async-start(bf16[64,8,128]{2,1,0:T(8,128)(2,1)} %bitcast.9), calls=%async_computation | async-start | bytes 262144 | tf_op jit(solution)/shard_map/all_to_all | solution.py:526
  18.6 0.0 copy-start
  18.6 3.6 %shard_map.128 = (bf16[512,128]{1,0:T(8,128)(2,1)}, bf16[128,1152]{1,0:T(8,128)(2,1)}, bf16[288,1024]{1,0:T(8,128)(2,1)S(1)}, bf16[1,4,1024]{2,1,0:T(4,128)(2,1)S(1)}) custom-call(bf16[1024,128]{1,0:T(8,128)(2,1)} %get-tuple-element.20.refs_0_.refs_5_, bf16[16,2048]{1,0:T(8,128)(2,1)} %refs_7_.1, bf16[1024,1024]{1,0:T(8,128)(2,1)} %refs_5_.1, ...), custom_call_target="tpu_custom_call" | custom-call | flops 999999995904 | bytes 3500000 | tf_op jit(solution)/shard_map/pallas_call | solution.py:470
  22.9 5.6 %all-to-all-done = bf16[64,8,128]{2,1,0:T(8,128)(2,1)} async-done(((bf16[64,8,128]{2,1,0:T(8,128)(2,1)}), bf16[64,8,128]{2,1,0:T(8,128)(2,1)}, u32[]{:S(2)}, u32[]{:S(2)}) %all-to-all-start) | async-done | bytes 131104 | tf_op jit(solution)/shard_map/all_to_all | solution.py:526
  28.5 0.0 copy-done
  28.5 0.0 copy-start.3
  28.5 0.0 copy-start.4
  28.5 4.0 %shard_map.129 = (bf16[1024,128]{1,0:T(8,128)(2,1)}, bf16[896,128]{1,0:T(8,128)(2,1)S(1)}, bf16[16,1024]{1,0:T(8,128)(2,1)S(1)}) custom-call(s32[1,4]{1,0:T(1,128)S(1)} %copy-done, s32[1]{0:T(128)S(6)} %copy.16.refs_1_, bf16[512,128]{1,0:T(8,128)(2,1)} %bitcast.1.refs_2_, bf16[288,1024]{1,0:T(8,128)(2,1)S(1)} %get-tuple-element.21.refs_3_, ...), custom_call_target="tpu_custom_call" | custom-call | flops 3999999983616 | bytes 14000000 | tf_op jit(solution)/shard_map/pallas_call | solution.py:470
  32.5 6.8 %all-to-all-start.1 = ((bf16[8,128,128]{2,1,0:T(8,128)(2,1)}), bf16[8,128,128]{2,1,0:T(8,128)(2,1)S(1)}, u32[]{:S(2)}, u32[]{:S(2)}) async-start(bf16[8,128,128]{2,1,0:T(8,128)(2,1)} %bitcast.8), calls=%async_computation.1 | async-start | bytes 524288 | tf_op jit(solution)/shard_map/all_to_all | solution.py:560
  39.3 4.2 %collective-permute-start.1 = (bf16[512,128]{1,0:T(8,128)(2,1)}, bf16[512,128]{1,0:T(8,128)(2,1)}, u32[]{:S(2)}, u32[]{:S(2)}) collective-permute-start(bf16[512,128]{1,0:T(8,128)(2,1)} %get-tuple-element.26), channel_id=1, source_target_pairs={{1,0},{2,1},{3,2},{4,3},{5,4},{6,5},{7,6},{8,7},{9,8},{10,9},{11,1... | collective-permute-start | bytes 393224 | tf_op jit(solution)/shard_map/ppermute | solution.py:548
  43.5 1.9 %collective-permute-start = (bf16[512,128]{1,0:T(8,128)(2,1)}, bf16[512,128]{1,0:T(8,128)(2,1)}, u32[]{:S(2)}, u32[]{:S(2)}) collective-permute-start(bf16[512,128]{1,0:T(8,128)(2,1)} %get-tuple-element.26), channel_id=1, source_target_pairs={{0,1},{1,2},{2,3},{3,4},{4,5},{5,6},{6,7},{7,8},{8,9},{9,10},{10,1... | collective-permute-start | bytes 393224 | tf_op jit(solution)/shard_map/ppermute | solution.py:547
  45.5 0.0 copy-done.3
  45.5 0.1 copy.15.refs_2_
  45.6 0.0 copy-done.4
  45.6 0.1 copy.14.refs_0_
  45.7 3.0 %all-to-all-done.1 = bf16[8,128,128]{2,1,0:T(8,128)(2,1)S(1)} async-done(((bf16[8,128,128]{2,1,0:T(8,128)(2,1)}), bf16[8,128,128]{2,1,0:T(8,128)(2,1)S(1)}, u32[]{:S(2)}, u32[]{:S(2)}) %all-to-all-start.1) | async-done | bytes 262176 | tf_op jit(solution)/shard_map/all_to_all | solution.py:560
  48.7 0.0 copy-start.1
  48.7 0.0 copy-start.2
  48.7 2.4 %shard_map.130 = bf16[1024,128]{1,0:T(8,128)(2,1)} custom-call(bf16[1024,128]{1,0:T(8,128)(2,1)S(1)} %bitcast.6, bf16[896,128]{1,0:T(8,128)(2,1)S(1)} %get-tuple-element.24.refs_1_, bf16[16,1024]{1,0:T(8,128)(2,1)S(1)} %get-tuple-element.25.refs_2_), custom_call_target="tpu_custom_call" | custom-call | flops 3000000053248 | bytes 10500000 | tf_op jit(solution)/shard_map/pallas_call | solution.py:470
  51.1 8.3 %all-to-all-start.2 = ((bf16[64,16,128]{2,1,0:T(8,128)(2,1)}), bf16[64,16,128]{2,1,0:T(8,128)(2,1)}, u32[]{:S(2)}, u32[]{:S(2)}) async-start(bf16[64,16,128]{2,1,0:T(8,128)(2,1)} %bitcast.7), calls=%async_computation.2 | async-start | bytes 524288 | tf_op jit(solution)/shard_map/all_to_all | solution.py:570
  59.4 0.0 collective-permute-done.1.refs_6_
  59.4 0.0 collective-permute-done.refs_4_
  59.4 0.0 copy-done.1
  59.4 0.0 copy-done.2
  59.4 7.7 %shard_map.131 = (bf16[1024,128]{1,0:T(8,128)(2,1)S(1)}, f32[16,2048]{1,0:T(8,128)S(1)}, bf16[128,1152]{1,0:T(8,128)(2,1)S(1)}, bf16[62,1024]{1,0:T(8,128)(2,1)S(1)}, bf16[32,2048]{1,0:T(8,128)(2,1)S(1)}) custom-call(s32[63,4]{1,0:T(8,128)S(1)} %copy.14.refs_0_, s32[63]{0:T(128)S(1)} %copy-done.1, s32[32,4]{1,0:T(8,128)S(1)} %copy.15.refs_2_, ...), custom_call_target="tpu_custom_call" | custom-call | flops 7999999967232 | bytes 28000000 | tf_op jit(solution)/shard_map/pallas_call | solution.py:470
  67.1 4.6 %all-to-all-done.2 = bf16[64,16,128]{2,1,0:T(8,128)(2,1)} async-done(((bf16[64,16,128]{2,1,0:T(8,128)(2,1)}), bf16[64,16,128]{2,1,0:T(8,128)(2,1)}, u32[]{:S(2)}, u32[]{:S(2)}) %all-to-all-start.2) | async-done | bytes 262176 | tf_op jit(solution)/shard_map/all_to_all | solution.py:570
  71.8 3.6 %shard_map.132 = bf16[16,2048]{1,0:T(8,128)(2,1)} custom-call(bf16[1024,128]{1,0:T(8,128)(2,1)} %bitcast.5.refs_0_, bf16[128,1152]{1,0:T(8,128)(2,1)S(1)} %get-tuple-element.28.refs_1_, bf16[1024,128]{1,0:T(8,128)(2,1)S(1)} %get-tuple-element.29.refs_2_, bf16[62,1024]{1,0:T(8,128)(2,1)S(1)} %get-tuple-element.30.refs_3_, ...), custom_call_target="tpu_custom_call" | custom-call | flops 3999999983616 | bytes 14000000 | tf_op jit(solution)/shard_map/pallas_call | solution.py:470
Async XLA Ops:
  3.6 24.9 %all-to-all-start = ((bf16[64,8,128]{2,1,0:T(8,128)(2,1)}), bf16[64,8,128]{2,1,0:T(8,128)(2,1)}, u32[]{:S(2)}, u32[]{:S(2)}) async-start(bf16[64,8,128]{2,1,0:T(8,128)(2,1)} %bitcast.9), calls=%async_computation | async-start | bytes 262144 | tf_op jit(solution)/shard_map/all_to_all | solution.py:526
  18.6 9.8 %copy-start = (s32[1,4]{1,0:T(1,128)S(1)}, s32[1,4]{1,0:T(1,128)}, u32[]{:S(2)}) copy-start(s32[1,4]{1,0:T(1,128)} %refs_0_.4) | copy-start | bytes 52
  28.5 17.0 %copy-start.3 = (s32[32,4]{0,1:T(4,128)S(1)}, s32[32,4]{0,1:T(4,128)}, u32[]{:S(2)}) copy-start(s32[32,4]{0,1:T(4,128)} %param.24) | copy-start | bytes 1540
  28.5 17.1 %copy-start.4 = (s32[63,4]{0,1:T(4,128)S(1)}, s32[63,4]{0,1:T(4,128)}, u32[]{:S(2)}) copy-start(s32[63,4]{0,1:T(4,128)} %param.18) | copy-start | bytes 3028
  32.5 16.2 %all-to-all-start.1 = ((bf16[8,128,128]{2,1,0:T(8,128)(2,1)}), bf16[8,128,128]{2,1,0:T(8,128)(2,1)S(1)}, u32[]{:S(2)}, u32[]{:S(2)}) async-start(bf16[8,128,128]{2,1,0:T(8,128)(2,1)} %bitcast.8), calls=%async_computation.1 | async-start | bytes 524288 | tf_op jit(solution)/shard_map/all_to_all | solution.py:560
  39.3 20.1 %collective-permute-start.1 = (bf16[512,128]{1,0:T(8,128)(2,1)}, bf16[512,128]{1,0:T(8,128)(2,1)}, u32[]{:S(2)}, u32[]{:S(2)}) collective-permute-start(bf16[512,128]{1,0:T(8,128)(2,1)} %get-tuple-element.26), channel_id=1, source_target_pairs={{1,0},{2,1},{3,2},{4,3},{5,4},{6,5},{7,6},{8,7},{9,8},{10,9},{11,1... | collective-permute-start | bytes 393224 | tf_op jit(solution)/shard_map/ppermute | solution.py:548
  43.5 15.9 %collective-permute-start = (bf16[512,128]{1,0:T(8,128)(2,1)}, bf16[512,128]{1,0:T(8,128)(2,1)}, u32[]{:S(2)}, u32[]{:S(2)}) collective-permute-start(bf16[512,128]{1,0:T(8,128)(2,1)} %get-tuple-element.26), channel_id=1, source_target_pairs={{0,1},{1,2},{2,3},{3,4},{4,5},{5,6},{6,7},{7,8},{8,9},{9,10},{10,1... | collective-permute-start | bytes 393224 | tf_op jit(solution)/shard_map/ppermute | solution.py:547
  48.7 10.7 %copy-start.1 = (s32[63]{0:T(128)S(1)}, s32[63]{0:T(128)}, u32[]{:S(2)}) copy-start(s32[63]{0:T(128)} %refs_1_.6) | copy-start | bytes 760
  48.7 10.7 %copy-start.2 = (s32[32]{0:T(128)S(1)}, s32[32]{0:T(128)}, u32[]{:S(2)}) copy-start(s32[32]{0:T(128)} %refs_3_.3) | copy-start | bytes 388
  51.1 20.7 %all-to-all-start.2 = ((bf16[64,16,128]{2,1,0:T(8,128)(2,1)}), bf16[64,16,128]{2,1,0:T(8,128)(2,1)}, u32[]{:S(2)}, u32[]{:S(2)}) async-start(bf16[64,16,128]{2,1,0:T(8,128)(2,1)} %bitcast.7), calls=%async_computation.2 | async-start | bytes 524288 | tf_op jit(solution)/shard_map/all_to_all | solution.py:570

commit v4 on v3

--- a/solution.py
+++ b/solution.py
@@ -53,11 +53,11 @@
 
 
 def up_levels(c, rows):
-    first, rest, fold = spread_matrix(False), spread_matrix(True), fold_matrix()
+    spread, fold = spread_matrix(), fold_matrix()
     levels = []
     n = c.shape[0] // 16
-    for i, e in enumerate(rows):
-        c = up_level(c, e, first if i == 0 else rest, n)
+    for e in rows:
+        c = up_level(c, e, spread, n)
         levels.append(dot(c, fold).astype(BF16))
         n //= 2
     return levels
@@ -80,6 +80,38 @@
     return jnp.concatenate(parts, 1).reshape(m * 32, 128)
 
 
+def down_levels(y, e, added, gather):
+    v = y.shape[0]
+    for h in range(LEVELS - 2, -1, -1):
+        n = LPD >> h
+        t = []
+        for j in range(n):
+            p = y[v * (j // 2) : v * (j // 2) + v]
+            row = e[OFFS[h] + j : OFFS[h] + j + 1]
+            t.append(
+                jnp.concatenate([p * row[:, 128 * m : 128 * m + 128] for m in range(8)], 1).astype(
+                    BF16
+                )
+            )
+        y = dot(jnp.concatenate(t, 0), gather)
+        if added is not None:
+            y = y + added[v * OFFS[h] : v * (OFFS[h] + n)]
+        y = y.astype(BF16).astype(F32)
+    return y
+
+
+def at_points(y, basis):
+    v = y.shape[0] // LPD
+    g = lanes((v, 128), 32)
+    out = []
+    for i in range(8):
+        t = y[4 * v * i : 4 * v * i + v]
+        for k in range(1, 4):
+            t = jnp.where(g == k, y[4 * v * i + v * k : 4 * v * i + v * k + v], t)
+        out.append(dot(t.astype(BF16), block_basis(basis, i).astype(BF16)))
+    return out
+
+
 def block_basis(basis, i):
     b = basis[:, 256 * i : 256 * i + 256]
     b = jnp.concatenate([b] * 4, 0)
@@ -95,9 +127,8 @@
     return jnp.where(cond, 1.0, 0.0).astype(BF16)
 
 
-def spread_matrix(parts):
-    r = iota((128, 1024), 0, 1)
-    return mask(iota((128, 1024), 1, 32) == (r % 32 if parts else r))
+def spread_matrix():
+    return mask(iota((128, 1024), 1, 32) == iota((128, 1024), 0, 1) % 32)
 
 
 def fold_matrix():
@@ -141,9 +172,9 @@
         )
         for k in range(4):
             rows.append(jnp.where(g == k, c, 0.0))
-    c = dot(jnp.concatenate(rows, 0).astype(BF16), fold).astype(BF16)
+    c = jnp.concatenate(rows, 0).astype(BF16)
     below = [e[OFFS[h] : OFFS[h] + (LPD >> h)] for h in range(LEVELS - 1)]
-    levels = [c] + up_levels(c, below)
+    levels = [dot(c, fold).astype(BF16)] + up_levels(c, below)
     root = levels[-1].astype(F32)
     g8 = lanes((8, 128), 32)
     msg = jnp.where(g8 == 0, root[0:8], jnp.where(g8 == 1, root[8:16], 0.0))
@@ -153,14 +184,16 @@
     stack_out[...] = jnp.concatenate(levels + [jnp.zeros((16, 128), BF16)], 0)
 
 
-def exchange_kernel(ready, stack, points, ex_out, chain_out, rows, low_rows):
+def exchange_kernel(
+    ready, stack, points, transfer, basis, ex_out, chain_out, nested_out, rows, low_rows
+):
     ready()
     ex_out[0:256] = pack(stack[...].astype(F32)).astype(BF16)
     for i in range(16):
         ex_out[256 + 16 * i : 272 + 16 * i] = points[:, 128 * i : 128 * i + 128]
     y, low = position()
     node = 512 + y * 64 + low
-    one, rest, fold = spread_matrix(False), spread_matrix(True), fold_matrix()
+    spread, fold = spread_matrix(), fold_matrix()
     q = mask(iota((32, 128), 0, 1) == iota((32, 128), 1, 1))
     for c in ready.rest:
         c.wait()
@@ -169,7 +202,7 @@
     low_rows[128:176] = rows[240:288].astype(F32)
     for d in range(9, 0, -1):
         at = jnp.right_shift(node, 9 - d)
-        t = dot(q, one if d == 9 else rest)
+        t = dot(q, spread)
         t = t * low_rows[pl.ds(at if d < 7 else 16 * d + at % 16 + 16, 1)]
         p = t[:, 0:128]
         for m in range(1, 8):
@@ -177,19 +210,21 @@
         q = p.astype(BF16)
         g = dot(q, fold).astype(BF16)
         chain_out[:, 128 * (d - 1) : 128 * d] = jnp.concatenate([g] * 4, 0)
+    one = jnp.where((iota((32, 128), 0, 1) - iota((32, 128), 1, 1)) % 32 == 0, 1.0, 0.0)
+    leaves = down_levels(one, transfer[...].astype(F32), None, gather_matrix())
+    for i, u in enumerate(at_points(leaves, basis[...].astype(F32))):
+        nested_out[:, 256 * i : 256 * i + 256] = u.astype(BF16)
 
 
 def plane_kernel(
     ready, index, count, arrived, rows, tops, msg_out, own_out, low_rows
 ):
-    pick = pick_matrix()
     y, low = position()
     node = y * 64 + low
     ready()
-    w = dot(arrived[...], pick[:, 0:256])
-    c = jnp.concatenate(
-        [w[:, 0:128].reshape(64, 1, 8, 128), w[:, 128:256].reshape(64, 1, 8, 128)], 1
-    )
+    c = arrived[...].astype(F32).reshape(64, 1, 8, 128)
+    g = lanes((64, 1, 8, 128), 32)
+    c = jnp.concatenate([jnp.where(g == 0, c, 0.0), jnp.where(g == 1, c, 0.0)], 1)
     c = c.reshape(1024, 128).astype(BF16)
     low_rows[...] = rows[0:128].astype(F32)
     e = [rows[176:240].astype(F32), rows[144:176].astype(F32), rows[128:144].astype(F32)]
@@ -227,13 +262,15 @@
         first = jnp.where((depth == d) & (low > 0), 1 << d, first)
     planes = (0, 1, 2 + y // 4, 4 + y // 2)
     places = (start + low - first, STARTS[6] + low % 8, STARTS[7] + low % 16, STARTS[8] + low % 32)
-    table[...] = jnp.zeros((NODES * 16, 128), F32)
     ready()
 
     def put(depth, place, value):
         s = (STARTS[depth] + place) * 16
         table[s : s + value.shape[0]] = value
 
+    for d in range(6):
+        put(d, 0, jnp.zeros((16 * REACH, 128), F32))
+        put(d, REACH + (1 << d), jnp.zeros((16 * REACH, 128), F32))
     d3 = []
     for p in range(8):
         c = unpack(arrived[MSG * p + 64 : MSG * p + 96], pick)
@@ -242,7 +279,7 @@
         put(5, REACH + 4 * p, c[48:112])
     c = jnp.concatenate(d3, 0)
     put(3, REACH, c)
-    c = c.astype(BF16)
+    c = jnp.where(lanes((128, 128), 32) == 0, c, 0.0).astype(BF16)
     e = rows[...].astype(F32)
     for d, c in zip((2, 1, 0), up_levels(c, [e[8:16], e[4:8], e[2:4]])):
         put(d, REACH, c.astype(F32))
@@ -281,9 +318,10 @@
     after,
     points,
     coupling,
+    transfer,
+    basis,
     block,
-    zl_out,
-    near_out,
+    out,
     table,
     prod,
     leaves,
@@ -293,7 +331,11 @@
     y, low = position()
     prior = y * 64 + low - 1
     prod[1008:1024] = jnp.zeros((16, 1024), BF16)
-    ready()
+    ready(0)
+    table[0:1024] = unpack(before[0:256], pick)
+    table[1024:2048] = stack[...].astype(F32)
+    table[2048:3072] = unpack(after[0:256], pick)
+    ready(1)
 
     window = [before[256:512]]
     window += [points[:, 128 * i : 128 * i + 128] for i in range(16)]
@@ -310,6 +352,34 @@
     four = jnp.concatenate([x.reshape(48, 1, 16, 128) for x in four], 1)
     leaves[0:3072] = four.reshape(3072, 128).astype(BF16)
     leaves[3072:3104] = jnp.zeros((32, 128), BF16)
+    def level(h):
+        n = LPD >> h
+
+        def step(t):
+            b = coupling[t].astype(F32)
+            acc = [None] * 8
+            for f in range(FAR):
+                at = far_index[t, f] - prior * n
+                at = at + OFFS[h] + (64 - n) * (
+                    (at >= n).astype(jnp.int32) + (at >= 2 * n).astype(jnp.int32)
+                )
+                at = jnp.where(f < far_count[t], at, 127) * 16
+                c = table[pl.ds(pl.multiple_of(at, 16), 16)]
+                for m in range(8):
+                    r = b[f : f + 1, 128 * m : 128 * m + 128] * c
+                    acc[m] = r if f == 0 else acc[m] + r
+            prod[pl.ds(pl.multiple_of(t * 16, 16), 16)] = jnp.concatenate(acc, 1).astype(BF16)
+
+        pl.loop(OFFS[h], OFFS[h] + n, unroll=min(n, 16))(step)
+
+    ready(2)
+    for h in range(LEVELS):
+        level(h)
+    zl = dot(prod[...], gather).astype(BF16).astype(F32)
+    ready(3, 4)
+    y = down_levels(zl[992:1008], transfer[...].astype(F32), zl, gather)
+    far = at_points(y, basis[...].astype(F32))
+    ready(5)
     slot = lanes((32, 128), 1) % NEAR
 
     def leaf(t):
@@ -334,45 +404,16 @@
         halves[at, 0:128] = q[0:16]
         halves[at, 128:256] = q[16:32]
 
-    pl.loop(0, LPD, unroll=4)(leaf)
+    pl.loop(0, LPD, unroll=32)(leaf)
     r = dot(halves[...], pair)
     g = lanes((16, 128), 64)
     for i in range(16):
-        near_out[:, 128 * i : 128 * i + 128] = jnp.where(
-            g == 0, r[32 * i : 32 * i + 16], r[32 * i + 16 : 32 * i + 32]
-        )
-
-    table[0:1024] = unpack(before[0:256], pick)
-    table[1024:2048] = stack[...].astype(F32)
-    table[2048:3072] = unpack(after[0:256], pick)
-
-    def level(h):
-        n = LPD >> h
-
-        def step(t):
-            b = coupling[t].astype(F32)
-            acc = [None] * 8
-            for f in range(FAR):
-                at = far_index[t, f] - prior * n
-                at = at + OFFS[h] + (64 - n) * (
-                    (at >= n).astype(jnp.int32) + (at >= 2 * n).astype(jnp.int32)
-                )
-                at = jnp.where(f < far_count[t], at, 127) * 16
-                c = table[pl.ds(pl.multiple_of(at, 16), 16)]
-                for m in range(8):
-                    r = b[f : f + 1, 128 * m : 128 * m + 128] * c
-                    acc[m] = r if f == 0 else acc[m] + r
-            prod[pl.ds(pl.multiple_of(t * 16, 16), 16)] = jnp.concatenate(acc, 1).astype(BF16)
-
-        pl.loop(OFFS[h], OFFS[h] + n, unroll=min(n, 4))(step)
-
-    for h in range(LEVELS):
-        level(h)
-    zl_out[...] = dot(prod[...], gather).astype(BF16)
-
-
-def down_kernel(ready, arrived, chain, zl, transfer, basis, near, out):
-    gather = gather_matrix()
+        near = jnp.where(g == 0, r[32 * i : 32 * i + 16], r[32 * i + 16 : 32 * i + 32])
+        own = far[i // 2][:, 128 * (i % 2) : 128 * (i % 2) + 128]
+        out[:, 128 * i : 128 * i + 128] = near + own
+
+
+def down_kernel(ready, arrived, chain, nested, rest, out):
     y, low = position()
     node = 512 + y * 64 + low
     ready()
@@ -392,31 +433,10 @@
         (((1,), (1,)), ((), ())),
         preferred_element_type=F32,
     )
-    zloc = zl[...].astype(F32)
-    y = (y + zloc[992:1008]).astype(BF16).astype(F32)
-
-    def spread_down(y, row):
-        return jnp.concatenate([y * row[:, 128 * m : 128 * m + 128] for m in range(8)], 1)
-
-    e = transfer[...].astype(F32)
-    for h in range(LEVELS - 2, -1, -1):
-        n = LPD >> h
-        t = [
-            spread_down(y[16 * (j // 2) : 16 * (j // 2) + 16], e[OFFS[h] + j : OFFS[h] + j + 1])
-            for j in range(n)
-        ]
-        t = jnp.concatenate(t, 0).astype(BF16)
-        zs = zloc[16 * OFFS[h] : 16 * (OFFS[h] + n)]
-        y = (dot(t, gather) + zs).astype(BF16).astype(F32)
-    bas = basis[...].astype(F32)
-    g = lanes((16, 128), 32)
+    y = y[:, 0:RANK].astype(BF16)
     for i in range(8):
-        t = y[64 * i : 64 * i + 16]
-        for k in range(1, 4):
-            t = jnp.where(g == k, y[64 * i + 16 * k : 64 * i + 16 * k + 16], t)
         s = slice(256 * i, 256 * i + 256)
-        far = dot(t.astype(BF16), block_basis(bas, i).astype(BF16))
-        out[:, s] = (far + near[:, s]).astype(BF16)
+        out[:, s] = (dot(y, nested[:, s]) + rest[:, s]).astype(BF16)
 
 
 def call(body, out, out_kinds, scratch, kinds, args, micros, direct=()):
@@ -455,9 +475,9 @@
         for c in copies + straight:
             c.start()
 
-        def ready():
-            for c in copies:
-                c.wait()
+        def ready(*which):
+            for i in which or range(len(copies)):
+                copies[i].wait()
 
         ready.rest = straight
         body(ready, *given, *own)
@@ -525,23 +545,24 @@
     )
     plane_roots = lax.all_to_all(root_msg, PLANE, 0, 0, tiled=True)
 
-    ex, chain, rows, tops = call(
+    ex, chain, nested, rows, tops = call(
         exchange_kernel,
-        [shape(512, 128), shape(128, 1152), shape(288, 1024)] + like(top_coupling),
-        "hhqr",
+        [shape(512, 128), shape(128, 1152), shape(RANK, LPD * LEAF), shape(288, 1024)]
+        + like(top_coupling),
+        "hhhqr",
         [pltpu.VMEM((176, 1024), F32)],
-        "hhrr",
-        (stack, points, top_transfer, top_coupling),
+        "hhhhrr",
+        (stack, points, transfer, basis, top_transfer, top_coupling),
         COST[1],
         direct=[
-            (2, 0, 128, 2, 0),
-            (2, lambda y, low: 128 + (y * 64 + low) // 4 // 16 * 16, 16, 2, 240),
-            (2, lambda y, low: 256 + (y * 64 + low) // 2 // 16 * 16, 16, 2, 256),
-            (2, lambda y, low: 512 + (y * 64 + low) // 16 * 16, 16, 2, 272),
-            (2, lambda y, low: 512 + 64 * y, 64, 2, 176),
-            (2, lambda y, low: 256 + 32 * y, 32, 2, 144),
-            (2, lambda y, low: 128 + 16 * y, 16, 2, 128),
-            (3, 0, 0, 3, 0),
+            (4, 0, 128, 3, 0),
+            (4, lambda y, low: 128 + (y * 64 + low) // 4 // 16 * 16, 16, 3, 240),
+            (4, lambda y, low: 256 + (y * 64 + low) // 2 // 16 * 16, 16, 3, 256),
+            (4, lambda y, low: 512 + (y * 64 + low) // 16 * 16, 16, 3, 272),
+            (4, lambda y, low: 512 + 64 * y, 64, 3, 176),
+            (4, lambda y, low: 256 + 32 * y, 32, 3, 144),
+            (4, lambda y, low: 128 + 16 * y, 16, 3, 128),
+            (5, 0, 0, 4, 0),
         ],
     )
     before = lax.ppermute(ex, ALL, [(i, i + 1) for i in range(devices - 1)])
@@ -568,17 +589,17 @@
         COST[3],
     )
     z_all = lax.all_to_all(z_msg, PLANE, 0, 0, tiled=True)
-    zl, near, held_chain, held_transfer, held_basis = call(
+    rest, held_chain, held_nested = call(
         side_kernel,
-        [shape(1024, 128), shape(VEC, LPD * LEAF, F32)] + like(chain, transfer, basis),
-        "vvrrr",
+        [shape(VEC, LPD * LEAF, F32)] + like(chain, nested),
+        "vrr",
         [
             pltpu.VMEM((3072, 128), F32),
             pltpu.VMEM((1024, 1024), BF16),
             pltpu.VMEM((3104, 128), BF16),
             pltpu.VMEM((512, 256), BF16),
         ],
-        "sssswhwhhhrrr",
+        "sssswhwhhhhhrr",
         (
             far_index,
             far_count,
@@ -589,21 +610,22 @@
             after,
             points,
             coupling,
+            transfer,
+            basis,
             near_block,
             chain,
-            transfer,
-            basis,
+            nested,
         ),
         COST[4],
-        direct=[(10, 0, 0, 2, 0), (11, 0, 0, 3, 0), (12, 0, 0, 4, 0)],
+        direct=[(12, 0, 0, 1, 0), (13, 0, 0, 2, 0)],
     )
     (result,) = call(
         down_kernel,
         [shape(VEC, LPD * LEAF)],
         "h",
         [],
-        "wvvvvv",
-        (z_all, held_chain, zl, held_transfer, held_basis, near),
+        "wvvv",
+        (z_all, held_chain, held_nested, rest),
         COST[6],
     )
     return result

time: 75.8 us -> 76.4 us (level)
  waiting for transfers between devices: 13.3 us -> 9.63 us
  starting transfers between devices: 36.3 us -> 39.1 us
  Pallas kernels: 24.8 us -> 26.1 us
    all_to_all x1, waiting for transfers between devices: 5.58 us -> 3.14 us  [local(): plane_roots = lax.all_to_all(root_msg, PLANE, 0, 0, tiled=True)]
    all_to_all x1, starting transfers between devices: 8.31 us -> 10.5 us  [local(): z_all = lax.all_to_all(z_msg, PLANE, 0, 0, tiled=True)]
    pallas_call x6, Pallas kernels: 24.8 us -> 26.1 us  [call(): pl.pallas_call(kernel, out_shape=[(pltpu.HBM if k == 'h' else pltpu.VMEM)...]
  transfers between devices with their start and end apart: 5 -> 5, of which waited for: 3 -> 3; matrix products, arithmetic and copies ran while one was open for 0% -> 0% of each run, Pallas kernels for 18% -> 22%
where the time goes in v4:
time: 76.4 us; the launch traced here: 76 us
  starting transfers between devices  39.1 us (51%)
  Pallas kernels  26.1 us (34%)
  waiting for transfers between devices  9.63 us (13%)
  between operations  0.93 us (1%)
    pallas_call x6, Pallas kernels, call(): pl.pallas_call(kernel, out_shape=[(pltpu.HBM if k == 'h' else pltpu.VMEM)...  26.1 us
    all_to_all x1, starting transfers between devices, local(): plane_roots = lax.all_to_all(root_msg, PLANE, 0, 0, tiled=True)  15 us
    all_to_all x1, starting transfers between devices, local(): z_all = lax.all_to_all(z_msg, PLANE, 0, 0, tiled=True)  10.5 us
    all_to_all x1, starting transfers between devices, local(): planes = lax.all_to_all(msg, 'y', 0, 0, tiled=True)  6.83 us
    ppermute x1, starting transfers between devices, local(): after = lax.ppermute(ex, ALL, [(i + 1, i) for i in range(devices - 1)])  4.58 us
    all_to_all x1, waiting for transfers between devices, local(): z_all = lax.all_to_all(z_msg, PLANE, 0, 0, tiled=True)  4.1 us
    all_to_all x1, waiting for transfers between devices, local(): plane_roots = lax.all_to_all(root_msg, PLANE, 0, 0, tiled=True)  3.14 us
    all_to_all x1, waiting for transfers between devices, local(): planes = lax.all_to_all(msg, 'y', 0, 0, tiled=True)  2.38 us
  transfers between devices with their start and end apart: 5, of which 3 were waited for; matrix products, arithmetic and copies ran while one was open for 0% of the time, Pallas kernels for 22%

profile of v4, /device:TPU:1, one launch (start us, length us, event | category | flops | bytes accessed | tf_op | source)
XLA Modules:
  0.0 76.0 jit_solution(11942182629990603624)
XLA Ops:
  0.0 3.6 %shard_map.127 = (bf16[512,128]{1,0:T(8,128)(2,1)}, bf16[1024,128]{1,0:T(8,128)(2,1)}) custom-call(bf16[16,2048]{1,0:T(8,128)(2,1)} %refs_7_.1, bf16[32,2048]{1,0:T(8,128)(2,1)} %refs_10_.1, bf16[62,1024]{1,0:T(8,128)(2,1)} %refs_9_.1), custom_call_target="tpu_custom_call" | custom-call | flops 3999999983616 | bytes 14000000 | tf_op jit(solution)/shard_map/pallas_call | solution.py:490
  3.6 15.0 %all-to-all-start = ((bf16[64,8,128]{2,1,0:T(8,128)(2,1)}), bf16[64,8,128]{2,1,0:T(8,128)(2,1)}, u32[]{:S(2)}, u32[]{:S(2)}) async-start(bf16[64,8,128]{2,1,0:T(8,128)(2,1)} %bitcast.9), calls=%async_computation | async-start | bytes 262144 | tf_op jit(solution)/shard_map/all_to_all | solution.py:546
  18.6 0.0 copy-start
  18.6 6.0 %shard_map.128 = (bf16[512,128]{1,0:T(8,128)(2,1)}, bf16[128,1152]{1,0:T(8,128)(2,1)}, bf16[32,2048]{1,0:T(8,128)(2,1)}, bf16[288,1024]{1,0:T(8,128)(2,1)S(1)}, bf16[1,4,1024]{2,1,0:T(4,128)(2,1)S(1)}) custom-call(bf16[1024,128]{1,0:T(8,128)(2,1)} %get-tuple-element.19.refs_0_.refs_5_, bf16[16,2048]{1,0:T(8,128)(2,1)} %refs_7_.1, bf16[62,1024]{1,0:T(8,128)(2,1)} %refs_9_.1, ...), custom_call_target="tpu_custom_call" | custom-call | flops 999999995904 | bytes 3500000 | tf_op jit(solution)/shard_map/pallas_call | solution.py:490
  25.3 3.1 %all-to-all-done = bf16[64,8,128]{2,1,0:T(8,128)(2,1)} async-done(((bf16[64,8,128]{2,1,0:T(8,128)(2,1)}), bf16[64,8,128]{2,1,0:T(8,128)(2,1)}, u32[]{:S(2)}, u32[]{:S(2)}) %all-to-all-start) | async-done | bytes 131104 | tf_op jit(solution)/shard_map/all_to_all | solution.py:546
  28.5 0.0 copy-done
  28.5 0.0 copy-start.3
  28.5 0.0 copy-start.4
  28.5 3.9 %shard_map.129 = (bf16[1024,128]{1,0:T(8,128)(2,1)}, bf16[896,128]{1,0:T(8,128)(2,1)S(1)}, bf16[16,1024]{1,0:T(8,128)(2,1)S(1)}) custom-call(s32[1,4]{1,0:T(1,128)S(1)} %copy-done, s32[1]{0:T(128)S(6)} %copy.16.refs_1_, bf16[512,128]{1,0:T(8,128)(2,1)} %bitcast.1.refs_2_, bf16[288,1024]{1,0:T(8,128)(2,1)S(1)} %get-tuple-element.20.refs_3_, ...), custom_call_target="tpu_custom_call" | custom-call | flops 3999999983616 | bytes 14000000 | tf_op jit(solution)/shard_map/pallas_call | solution.py:490
  32.4 6.8 %all-to-all-start.1 = ((bf16[8,128,128]{2,1,0:T(8,128)(2,1)}), bf16[8,128,128]{2,1,0:T(8,128)(2,1)S(1)}, u32[]{:S(2)}, u32[]{:S(2)}) async-start(bf16[8,128,128]{2,1,0:T(8,128)(2,1)} %bitcast.8), calls=%async_computation.1 | async-start | bytes 524288 | tf_op jit(solution)/shard_map/all_to_all | solution.py:581
  39.2 2.2 %collective-permute-start = (bf16[512,128]{1,0:T(8,128)(2,1)}, bf16[512,128]{1,0:T(8,128)(2,1)}, u32[]{:S(2)}, u32[]{:S(2)}) collective-permute-start(bf16[512,128]{1,0:T(8,128)(2,1)} %get-tuple-element.25), channel_id=1, source_target_pairs={{0,1},{1,2},{2,3},{3,4},{4,5},{5,6},{6,7},{7,8},{8,9},{9,10},{10,1... | collective-permute-start | bytes 393224 | tf_op jit(solution)/shard_map/ppermute | solution.py:568
  41.4 4.6 %collective-permute-start.1 = (bf16[512,128]{1,0:T(8,128)(2,1)}, bf16[512,128]{1,0:T(8,128)(2,1)}, u32[]{:S(2)}, u32[]{:S(2)}) collective-permute-start(bf16[512,128]{1,0:T(8,128)(2,1)} %get-tuple-element.25), channel_id=1, source_target_pairs={{1,0},{2,1},{3,2},{4,3},{5,4},{6,5},{7,6},{8,7},{9,8},{10,9},{11,1... | collective-permute-start | bytes 393224 | tf_op jit(solution)/shard_map/ppermute | solution.py:569
  46.0 0.0 copy-done.3
  46.0 0.1 copy.14.refs_0_
  46.1 0.0 copy-done.4
  46.1 0.1 copy.15.refs_2_
  46.2 2.4 %all-to-all-done.1 = bf16[8,128,128]{2,1,0:T(8,128)(2,1)S(1)} async-done(((bf16[8,128,128]{2,1,0:T(8,128)(2,1)}), bf16[8,128,128]{2,1,0:T(8,128)(2,1)S(1)}, u32[]{:S(2)}, u32[]{:S(2)}) %all-to-all-start.1) | async-done | bytes 262176 | tf_op jit(solution)/shard_map/all_to_all | solution.py:581
  48.6 0.0 copy-start.1
  48.6 0.0 copy-start.2
  48.6 2.4 %shard_map.130 = bf16[1024,128]{1,0:T(8,128)(2,1)} custom-call(bf16[1024,128]{1,0:T(8,128)(2,1)S(1)} %bitcast.6, bf16[896,128]{1,0:T(8,128)(2,1)S(1)} %get-tuple-element.23.refs_1_, bf16[16,1024]{1,0:T(8,128)(2,1)S(1)} %get-tuple-element.24.refs_2_), custom_call_target="tpu_custom_call" | custom-call | flops 3000000053248 | bytes 10500000 | tf_op jit(solution)/shard_map/pallas_call | solution.py:490
  51.0 10.5 %all-to-all-start.2 = ((bf16[64,16,128]{2,1,0:T(8,128)(2,1)}), bf16[64,16,128]{2,1,0:T(8,128)(2,1)}, u32[]{:S(2)}, u32[]{:S(2)}) async-start(bf16[64,16,128]{2,1,0:T(8,128)(2,1)} %bitcast.7), calls=%async_computation.2 | async-start | bytes 524288 | tf_op jit(solution)/shard_map/all_to_all | solution.py:591
  61.4 0.0 collective-permute-done.refs_4_
  61.5 0.0 collective-permute-done.1.refs_6_
  61.5 0.0 copy-done.1
  61.5 0.0 copy-done.2
  61.5 8.0 %shard_map.131 = (f32[16,2048]{1,0:T(8,128)S(1)}, bf16[128,1152]{1,0:T(8,128)(2,1)S(1)}, bf16[32,2048]{1,0:T(8,128)(2,1)S(1)}) custom-call(s32[63,4]{1,0:T(8,128)S(1)} %copy.14.refs_0_, s32[63]{0:T(128)S(1)} %copy-done.1, s32[32,4]{1,0:T(8,128)S(1)} %copy.15.refs_2_, s32[32]{0:T(128)S(1)} %copy-done.2, bf16[512,128]{1,0:T(8,128)(2,1)} %collective-permute-done.refs_4_, ...), custom_call_target="tpu_custom_call" | custom-call | flops 7999999967232 | bytes 28000000 | tf_op jit(solution)/shard_map/pallas_call | solution.py:490
  69.5 4.1 %all-to-all-done.2 = bf16[64,16,128]{2,1,0:T(8,128)(2,1)} async-done(((bf16[64,16,128]{2,1,0:T(8,128)(2,1)}), bf16[64,16,128]{2,1,0:T(8,128)(2,1)}, u32[]{:S(2)}, u32[]{:S(2)}) %all-to-all-start.2) | async-done | bytes 262176 | tf_op jit(solution)/shard_map/all_to_all | solution.py:591
  73.6 2.2 %shard_map.132 = bf16[16,2048]{1,0:T(8,128)(2,1)} custom-call(bf16[1024,128]{1,0:T(8,128)(2,1)} %bitcast.5.refs_0_, bf16[128,1152]{1,0:T(8,128)(2,1)S(1)} %get-tuple-element.28.refs_1_, bf16[32,2048]{1,0:T(8,128)(2,1)S(1)} %get-tuple-element.29.refs_2_, f32[16,2048]{1,0:T(8,128)S(1)} %get-tuple-element.30.refs_3_), custom_call_target="tpu_custom_call" | custom-call | flops 3999999983616 | bytes 14000000 | tf_op jit(solution)/shard_map/pallas_call | solution.py:490
Async XLA Ops:
  3.6 24.9 %all-to-all-start = ((bf16[64,8,128]{2,1,0:T(8,128)(2,1)}), bf16[64,8,128]{2,1,0:T(8,128)(2,1)}, u32[]{:S(2)}, u32[]{:S(2)}) async-start(bf16[64,8,128]{2,1,0:T(8,128)(2,1)} %bitcast.9), calls=%async_computation | async-start | bytes 262144 | tf_op jit(solution)/shard_map/all_to_all | solution.py:546
  18.6 9.8 %copy-start = (s32[1,4]{1,0:T(1,128)S(1)}, s32[1,4]{1,0:T(1,128)}, u32[]{:S(2)}) copy-start(s32[1,4]{1,0:T(1,128)} %refs_0_.4) | copy-start | bytes 52
  28.5 17.5 %copy-start.3 = (s32[63,4]{0,1:T(4,128)S(1)}, s32[63,4]{0,1:T(4,128)}, u32[]{:S(2)}) copy-start(s32[63,4]{0,1:T(4,128)} %param.18) | copy-start | bytes 3028
  28.5 17.6 %copy-start.4 = (s32[32,4]{0,1:T(4,128)S(1)}, s32[32,4]{0,1:T(4,128)}, u32[]{:S(2)}) copy-start(s32[32,4]{0,1:T(4,128)} %param.24) | copy-start | bytes 1540
  32.4 16.2 %all-to-all-start.1 = ((bf16[8,128,128]{2,1,0:T(8,128)(2,1)}), bf16[8,128,128]{2,1,0:T(8,128)(2,1)S(1)}, u32[]{:S(2)}, u32[]{:S(2)}) async-start(bf16[8,128,128]{2,1,0:T(8,128)(2,1)} %bitcast.8), calls=%async_computation.1 | async-start | bytes 524288 | tf_op jit(solution)/shard_map/all_to_all | solution.py:581
  39.2 22.2 %collective-permute-start = (bf16[512,128]{1,0:T(8,128)(2,1)}, bf16[512,128]{1,0:T(8,128)(2,1)}, u32[]{:S(2)}, u32[]{:S(2)}) collective-permute-start(bf16[512,128]{1,0:T(8,128)(2,1)} %get-tuple-element.25), channel_id=1, source_target_pairs={{0,1},{1,2},{2,3},{3,4},{4,5},{5,6},{6,7},{7,8},{8,9},{9,10},{10,1... | collective-permute-start | bytes 393224 | tf_op jit(solution)/shard_map/ppermute | solution.py:568
  41.4 20.1 %collective-permute-start.1 = (bf16[512,128]{1,0:T(8,128)(2,1)}, bf16[512,128]{1,0:T(8,128)(2,1)}, u32[]{:S(2)}, u32[]{:S(2)}) collective-permute-start(bf16[512,128]{1,0:T(8,128)(2,1)} %get-tuple-element.25), channel_id=1, source_target_pairs={{1,0},{2,1},{3,2},{4,3},{5,4},{6,5},{7,6},{8,7},{9,8},{10,9},{11,1... | collective-permute-start | bytes 393224 | tf_op jit(solution)/shard_map/ppermute | solution.py:569
  48.6 12.9 %copy-start.1 = (s32[63]{0:T(128)S(1)}, s32[63]{0:T(128)}, u32[]{:S(2)}) copy-start(s32[63]{0:T(128)} %refs_1_.6) | copy-start | bytes 760
  48.6 12.9 %copy-start.2 = (s32[32]{0:T(128)S(1)}, s32[32]{0:T(128)}, u32[]{:S(2)}) copy-start(s32[32]{0:T(128)} %refs_3_.3) | copy-start | bytes 388
  51.0 22.7 %all-to-all-start.2 = ((bf16[64,16,128]{2,1,0:T(8,128)(2,1)}), bf16[64,16,128]{2,1,0:T(8,128)(2,1)}, u32[]{:S(2)}, u32[]{:S(2)}) async-start(bf16[64,16,128]{2,1,0:T(8,128)(2,1)} %bitcast.7), calls=%async_computation.2 | async-start | bytes 524288 | tf_op jit(solution)/shard_map/all_to_all | solution.py:591
